TPU v7x, 32 devices: a whole 2x2x4 slice. The times are simulated.
32 devices in a mesh: groups: 2 (over y), gx: 4 (over z), gy: 2 (over x), gz: 2 (over core).
Axes of the slice: x: 2, y: 2, z: 4, core: 2. Of those that a mesh axis runs over, the one named last changes fastest.
Arguments:
- stream: float32 [256, 64, 512], P('groups', 'gx', 'gy'), parts along dimension 0, may hold values from -6 to 6
- inductance: bfloat16 [16, 32, 8, 2, 128, 128], P(('groups', 'gx'), ('gy', 'gz')), parts along dimension 0, may hold values from -0.25 to 1.25
- near_lists: int32 [16, 32, 8], P(('groups', 'gx'), ('gy', 'gz')), parts along dimension 0, may hold values from 0 to 8, as said below
- filament_leaf: int32 [16384], P(('groups', 'gx', 'gy', 'gz')), parts along dimension 0, may hold values from 0 to 255, as said below
- filament_current: bfloat16 [16384, 128], P(('groups', 'gx', 'gy', 'gz')), parts along dimension 0, may hold values from -6 to 6
- filament_coupling: bfloat16 [16384, 2, 128], P(('groups', 'gx', 'gy', 'gz')), parts along dimension 0, may hold values from -0.75 to 0.75
Outputs:
- loop_voltage: float32 [256, 64, 512], P('groups', 'gx', ('gy', 'gz')), parts along dimension 0
- filament_voltage: bfloat16 [16384, 128], P(('groups', 'gx', 'gy', 'gz')), parts along dimension 0
There are 2 independent parts, one for each index of `groups`. A program takes and returns all parts, laid end to end along the dimension named above; each array names one. Nothing has to cross between parts.
Inputs may be any that keep to these rules, and one draw needn't show every extreme that they name: `near_lists`: entry 0 of every list is 4, the leaf itself; code k names the leaf k // 3 - 1 rows and k % 3 - 1 columns away, and repeats may occur. `filament_leaf`: leaves are numbered row by row over 8 x 32. Device d along gx+gy+gz holds the 2 x 8 leaves of leaf rows (d // (2 * 2)) * 2 on and leaf columns (d % (2 * 2)) * 8 on. Of the 512 filaments of one device, at most 64 lie over the leaves of any one device, and in every device's block some device gets exactly 64.
All inputs are finite; a program needn't handle non-finite values.
Results may differ from a plain program's by a relative error of at most 0.0049.
Values may be sent and summed in bfloat16 or wider, within the bound.
A program may use at most 128 MiB of HBM per device.

v0:
```python
import jax
import jax.numpy as jnp
from jax import lax
from jax.sharding import PartitionSpec as P

LEAF_R = 8
LEAF_C = 16


def with_halo(value, sides, width):
    for axis, dim in sides:
        size, length = (lax.axis_size(axis), value.shape[dim])
        up = [(i, (i + 1) % size) for i in range(size - 1)]
        down = [(j, i) for i, j in up]
        last = lax.slice_in_dim(value, length - width, length, axis=dim)
        leading = lax.slice_in_dim(value, 0, width, axis=dim)
        before = lax.ppermute(last, axis, up)
        after = lax.ppermute(leading, axis, down)
        value = jnp.concatenate([before, value, after], axis=dim)
    return value


def plane_curl(padded):
    along_y = padded[:, 1:-1, 2:] - padded[:, 1:-1, :-2]
    along_x = padded[:, :-2, 1:-1] - padded[:, 2:, 1:-1]
    return jnp.stack([along_y, along_x])


def to_leaves(grid_values):
    components, port_count, row_count, col_count = grid_values.shape
    blocks = grid_values.reshape(
        components, port_count, row_count // LEAF_R, LEAF_R, col_count // LEAF_C, LEAF_C
    )
    blocks = blocks.transpose(2, 4, 0, 1, 3, 5)
    return blocks.reshape(
        row_count // LEAF_R, col_count // LEAF_C, components, port_count, LEAF_R * LEAF_C
    )


def from_leaves(leaves):
    leaf_rows, leaf_cols, components, port_count, leaf_cells = leaves.shape
    blocks = leaves.reshape(leaf_rows, leaf_cols, components, port_count, LEAF_R, LEAF_C)
    blocks = blocks.transpose(2, 3, 0, 4, 1, 5)
    return blocks.reshape(components, port_count, leaf_rows * LEAF_R, leaf_cols * LEAF_C)


def body(stream, inductance, near_lists, filament_leaf, filament_current, filament_coupling):
    port_count = stream.shape[0]
    leaf_rows = inductance.shape[0]
    leaf_cols = inductance.shape[1]
    near_count = inductance.shape[2]
    leaf_cells = inductance.shape[4]
    leaf_count = leaf_rows * leaf_cols
    half_cols = leaf_cols * LEAF_C
    core_count = lax.axis_size("gz")
    core_index = lax.axis_index("gz")
    first_col = core_index * half_cols
    padded = with_halo(stream, (("gx", 1), ("gy", 2)), 1)
    window = lax.dynamic_slice_in_dim(padded, first_col, half_cols + 2, 2)
    currents = plane_curl(window).astype(jnp.bfloat16)
    bordered = with_halo(to_leaves(currents), (("gx", 0), (("gy", "gz"), 1)), 1)
    row_stride = leaf_cols + 2
    flattened = bordered.reshape((leaf_rows + 2) * row_stride, 2, port_count, leaf_cells)
    row_shift = near_lists // 3 - 1
    col_shift = near_lists % 3 - 1
    source = (jnp.arange(leaf_rows, dtype=jnp.int32)[:, None, None] + 1 + row_shift) * row_stride
    source = source + jnp.arange(leaf_cols, dtype=jnp.int32)[None, :, None] + 1 + col_shift
    sources = jnp.take(flattened, source.reshape(-1), axis=0).reshape(
        leaf_count, near_count, 2, port_count, leaf_cells
    )
    kernels = inductance.reshape(leaf_count, near_count, 2, leaf_cells, leaf_cells)
    near_field = lax.dot_general(
        sources, kernels, (((1, 4), (1, 4)), ((0, 2), (0, 2))), preferred_element_type=jnp.float32
    )
    own_leaves = bordered[1:-1, 1:-1].reshape(leaf_count, 2, port_count, leaf_cells)
    owners = lax.axis_size("gx") * lax.axis_size("gy") * core_count
    filament_count = filament_leaf.shape[0]
    capacity = max(2, 2 * filament_count // owners)
    slot_count = owners * capacity
    plane_cols = leaf_cols * lax.axis_size("gy") * core_count
    leaf_row = filament_leaf // plane_cols
    leaf_col = filament_leaf % plane_cols
    owner_ids = leaf_row // leaf_rows * (lax.axis_size("gy") * core_count) + leaf_col // leaf_cols
    local_ids = leaf_row % leaf_rows * leaf_cols + leaf_col % leaf_cols
    owner_hits = (owner_ids[:, None] == jnp.arange(owners, dtype=jnp.int32)[None, :]).astype(
        jnp.int32
    )
    position = jnp.sum((jnp.cumsum(owner_hits, axis=0) - 1) * owner_hits, axis=1)
    target_slot = owner_ids * capacity + position
    placement_mask = target_slot[None, :] == jnp.arange(slot_count, dtype=jnp.int32)[:, None]
    placement = placement_mask.astype(jnp.bfloat16)
    coupling_rows = filament_coupling.reshape(filament_count, 2 * leaf_cells)
    sent_coupling = jnp.dot(placement, coupling_rows, preferred_element_type=jnp.float32).astype(
        jnp.bfloat16
    )
    sent_current = jnp.dot(placement, filament_current, preferred_element_type=jnp.float32).astype(
        jnp.bfloat16
    )
    sent_leaf = jnp.max(jnp.where(placement_mask, local_ids[None, :], -1), axis=1)
    send_coupling = sent_coupling.reshape(owners, capacity, 2 * leaf_cells)
    send_current = sent_current.reshape(owners, capacity, port_count)
    send_leaf = sent_leaf.reshape(owners, capacity)
    got_coupling, got_current, got_leaf = (
        lax.all_to_all(send_coupling, ("gx", "gy", "gz"), split_axis=0, concat_axis=0, tiled=True),
        lax.all_to_all(send_current, ("gx", "gy", "gz"), split_axis=0, concat_axis=0, tiled=True),
        lax.all_to_all(send_leaf, ("gx", "gy", "gz"), split_axis=0, concat_axis=0, tiled=True),
    )
    got_coupling = got_coupling.reshape(slot_count, 2 * leaf_cells)
    got_current = got_current.reshape(slot_count, port_count)
    got_leaf = got_leaf.reshape(slot_count)
    leaf_hits = (got_leaf[:, None] == jnp.arange(leaf_count, dtype=jnp.int32)[None, :]).astype(
        jnp.bfloat16
    )
    spread = (leaf_hits[:, :, None] * got_coupling[:, None, :]).reshape(
        slot_count, leaf_count * 2 * leaf_cells
    )
    filament_field = lax.dot_general(
        got_current, spread, (((0,), (0,)), ((), ())), preferred_element_type=jnp.float32
    )
    filament_field = filament_field.reshape(port_count, leaf_count, 2, leaf_cells).transpose(
        1, 2, 0, 3
    )
    plane_rows = own_leaves.transpose(2, 0, 1, 3).reshape(port_count, leaf_count * 2 * leaf_cells)
    induced = lax.dot_general(
        spread, plane_rows, (((1,), (1,)), ((), ())), preferred_element_type=jnp.float32
    ).astype(jnp.bfloat16)
    returned = lax.all_to_all(
        induced.reshape(owners, capacity, port_count),
        ("gx", "gy", "gz"),
        split_axis=0,
        concat_axis=0,
        tiled=True,
    )
    returned = returned.reshape(slot_count, port_count)
    filament_voltage = lax.dot_general(
        placement, returned, (((0,), (0,)), ((), ())), preferred_element_type=jnp.float32
    ).astype(jnp.bfloat16)
    total_field = (near_field + filament_field).astype(jnp.bfloat16)
    grid_field = from_leaves(total_field.reshape(leaf_rows, leaf_cols, 2, port_count, leaf_cells))
    bordered_field = with_halo(grid_field, (("gx", 2), (("gy", "gz"), 3)), 1)
    x_field = bordered_field[0].astype(jnp.float32)
    y_field = bordered_field[1].astype(jnp.float32)
    loop_voltage = (
        x_field[:, 1:-1, :-2]
        - x_field[:, 1:-1, 2:]
        + (y_field[:, 2:, 1:-1] - y_field[:, :-2, 1:-1])
    )
    return (loop_voltage, filament_voltage)


def solution(mesh):
    return jax.shard_map(
        body,
        mesh=mesh,
        in_specs=(
            P("groups", "gx", "gy"),
            P(("groups", "gx"), ("gy", "gz"), None, None, None, None),
            P(("groups", "gx"), ("gy", "gz"), None),
            P(("groups", "gx", "gy", "gz")),
            P(("groups", "gx", "gy", "gz"), None),
            P(("groups", "gx", "gy", "gz"), None, None),
        ),
        out_specs=(P("groups", "gx", ("gy", "gz")), P(("groups", "gx", "gy", "gz"), None)),
        check_vma=False,
    )
```

profile of v0, /device:TPU:0, one launch (start us, length us, event | category | flops | bytes accessed | tf_op | source)
XLA Modules:
  0.0 139.7 jit_solution(7152915620468083119)
XLA Ops:
  4.0 7.4 %all-to-all-start.1 = ((s32[16,1,64]{2,1,0:T(1,128)}), s32[16,1,64]{2,1,0:T(1,128)S(1)}, u32[]{:S(2)}, u32[]{:S(2)}) async-start(s32[16,1,64]{2,1,0:T(1,128)} %all_to_all.16), calls=%async_computation.1 | async-start | bytes 16384 | tf_op jit(solution)/shard_map/all_to_all | solution.py:106
  11.3 2.0 %copy.46 = f32[128,16,256]{0,2,1:T(8,128)S(1)} copy(f32[128,16,256]{2,1,0:T(8,128)} %param.6) | data formatting | bytes 4194304 | tf_op args[0]
  13.3 3.8 %collective-permute-start = (f32[128,1,256]{0,2,1:T(8,128)S(1)}, f32[128,1,256]{0,2,1:T(8,128)S(1)}, u32[]{:S(2)}, u32[]{:S(2)}) collective-permute-start(f32[128,1,256]{0,2,1:T(8,128)S(1)} %get-tuple-element.12), channel_id=1, source_target_pairs={{0,4},{4,8},{8,12},{1,5},{5,9},{9,13},{2,6},{6,10},{10,14},{3,7},{... | collective-permute-start | bytes 393224 | tf_op jit(solution)/shard_map/ppermute | solution.py:17
  17.2 1.3 collective-permute-start.1
  18.5 1.4 fusion.11
  21.0 3.3 %collective-permute-done.1 = f32[128,1,256]{0,2,1:T(8,128)S(1)} collective-permute-done((f32[128,1,256]{0,2,1:T(8,128)S(1)}, f32[128,1,256]{0,2,1:T(8,128)S(1)}, u32[]{:S(2)}, u32[]{:S(2)}) %collective-permute-start.1) | collective-permute-done | bytes 131104 | tf_op jit(solution)/shard_map/ppermute | solution.py:18
  24.4 1.3 collective-permute-start.3
  25.7 4.5 %collective-permute-start.2 = (f32[128,18,1]{0,2,1:T(1,128)S(1)}, f32[128,18,1]{0,2,1:T(1,128)S(1)}, u32[]{:S(2)}, u32[]{:S(2)}) collective-permute-start(f32[128,18,1]{0,2,1:T(1,128)S(1)} %get-tuple-element.9), channel_id=1, source_target_pairs={{0,2},{1,3},{4,6},{5,7},{8,10},{9,11},{12,14},{13,15},{16,18},{17,... | collective-permute-start | bytes 27656 | tf_op jit(solution)/shard_map/ppermute | solution.py:17
  35.7 4.6 %collective-permute-start.4 = (bf16[1,8,2,128,128]{3,4,2,1,0:T(8,128)(2,1)}, bf16[1,8,2,128,128]{3,4,2,1,0:T(8,128)(2,1)S(1)}, u32[]{:S(2)}, u32[]{:S(2)}) collective-permute-start(bf16[1,8,2,128,128]{3,4,2,1,0:T(8,128)(2,1)} %bitcast.4), channel_id=1, source_target_pairs={{0,4},{4,8},{8,12},{1,5},{5,9},{9,13},{2,6},{6,10},{10,14},{3,7},{... | collective-permute-start | bytes 1572872 | tf_op jit(solution)/shard_map/ppermute | solution.py:17
  40.5 5.5 %all-to-all-start.2 = ((bf16[16,64,256]{2,1,0:T(8,128)(2,1)}), bf16[16,64,256]{2,1,0:T(8,128)(2,1)}, u32[]{:S(2)}, u32[]{:S(2)}) async-start(bf16[16,64,256]{2,1,0:T(8,128)(2,1)} %bitcast.19), calls=%async_computation.2 | async-start | bytes 1048576 | tf_op jit(solution)/shard_map/all_to_all | solution.py:104
  46.3 1.8 %collective-permute-done.5 = bf16[1,8,2,128,128]{3,4,2,1,0:T(8,128)(2,1)S(1)} collective-permute-done((bf16[1,8,2,128,128]{3,4,2,1,0:T(8,128)(2,1)}, bf16[1,8,2,128,128]{3,4,2,1,0:T(8,128)(2,1)S(1)}, u32[]{:S(2)}, u32[]{:S(2)}) %collective-permute-start.5) | collective-permute-done | bytes 524320 | tf_op jit(solution)/shard_map/ppermute | solution.py:18
  48.2 3.6 %collective-permute-done.4 = bf16[1,8,2,128,128]{3,4,2,1,0:T(8,128)(2,1)S(1)} collective-permute-done((bf16[1,8,2,128,128]{3,4,2,1,0:T(8,128)(2,1)}, bf16[1,8,2,128,128]{3,4,2,1,0:T(8,128)(2,1)S(1)}, u32[]{:S(2)}, u32[]{:S(2)}) %collective-permute-start.4) | collective-permute-done | bytes 524320 | tf_op jit(solution)/shard_map/ppermute | solution.py:17
  51.8 1.3 collective-permute-start.6
  53.1 1.3 collective-permute-start.7
  55.8 3.3 %collective-permute-done.7 = bf16[4,1,2,128,128]{3,4,2,1,0:T(8,128)(2,1)S(1)} collective-permute-done((bf16[4,1,2,128,128]{3,4,2,1,0:T(8,128)(2,1)S(1)}, bf16[4,1,2,128,128]{3,4,2,1,0:T(8,128)(2,1)S(1)}, u32[]{:S(2)}, u32[]{:S(2)}) %collective-permute-start.7) | collective-permute-done | bytes 262176 | tf_op jit(solution)/shard_map/ppermute | solution.py:18
  59.1 1.8 %pad_maximum_fusion = bf16[4,10,2,128,128]{3,4,2,1,0:T(8,128)(2,1)} fusion(bf16[4,1,2,128,128]{3,4,2,1,0:T(8,128)(2,1)S(1)} %collective-permute-done.7, bf16[1,8,2,128,128]{3,4,2,1,0:T(8,128)(2,1)S(1)} %collective-permute-done.5, bf16[2,8,2,128,128]{3,4,2,1,0:T(8,128)(2,1)S(1)} %bitcast.90, bf16[1,8,2,128,128]{3,4,2,1,0:T(8,128)(2,1)S(1)} %collective-permute-done.4, ...), kind=kLoop, calls=%fused_computation.6 | loop fusion | flops 5242880 | bytes 5242880 | tf_op jit(solution)/shard_map/concatenate | solution.py:19
  60.8 3.2 %copy.52 = bf16[4,10,2,128,128]{4,3,2,1,0:T(8,128)(2,1)S(1)} copy(bf16[4,10,2,128,128]{3,4,2,1,0:T(8,128)(2,1)} %pad_maximum_fusion) | data formatting | bytes 5242880 | tf_op jit(solution)/shard_map/concatenate | solution.py:19
  64.1 6.6 %gather_fusion = bf16[128,2,128,128]{3,2,1,0:T(8,128)(2,1)} fusion(bf16[40,2,128,128]{3,2,1,0:T(8,128)(2,1)S(1)} %bitcast.81, s32[1024]{0:T(1024)S(1)} %pad_clamp_fusion), kind=kCustom, calls=%fused_computation | custom fusion | bytes 16777728 | tf_op jit(solution)/shard_map/jit(_take)/gather | solution.py:68
  70.6 13.3 %all-to-all-start = ((bf16[16,64,128]{2,1,0:T(8,128)(2,1)}), bf16[16,64,128]{2,1,0:T(8,128)(2,1)S(1)}, u32[]{:S(2)}, u32[]{:S(2)}) async-start(bf16[16,64,128]{2,1,0:T(8,128)(2,1)} %bitcast.15), calls=%async_computation | async-start | bytes 524288 | tf_op jit(solution)/shard_map/all_to_all | solution.py:105
  85.1 3.9 %broadcast_multiply_fusion = bf16[1024,16,256]{0,2,1:T(8,128)(2,1)} fusion(bf16[1024,256]{0,1:T(8,128)(2,1)S(1)} %copy.56, bf16[1024,16]{0,1:T(8,128)(2,1)S(1)} %fusion.28), kind=kLoop, calls=%fused_computation.5 | loop fusion | flops 4194304 | bytes 8945664 | tf_op jit(solution)/shard_map/mul | solution.py:114
  89.1 4.9 %all-to-all-done = bf16[16,64,128]{2,1,0:T(8,128)(2,1)S(1)} async-done(((bf16[16,64,128]{2,1,0:T(8,128)(2,1)}), bf16[16,64,128]{2,1,0:T(8,128)(2,1)S(1)}, u32[]{:S(2)}, u32[]{:S(2)}) %all-to-all-start) | async-done | bytes 262176 | tf_op jit(solution)/shard_map/all_to_all | solution.py:105
  93.9 5.9 %fusion.51 = f32[128,16,2,128]{0,3,2,1:T(8,128)S(1)} fusion(bf16[1024,128,1,1]{1,0,3,2:T(8,128)(2,1)S(1)} %bitcast.96, bf16[16,2,128,1024]{3,2,1,0:T(8,128)(2,1)} %bitcast.82), kind=kOutput, calls=%fused_computation.114 | convolution fusion | flops 1073741824 | bytes 10747904 | tf_op jit(solution)/shard_map/dot_general | solution.py:117
  99.8 7.7 %fusion.3 = bf16[16,2,128,128]{2,3,1,0:T(8,128)(2,1)S(1)} fusion(f32[128,16,2,128]{0,3,2,1:T(8,128)S(1)} %fusion.51, bf16[16,8,2,128,128]{4,3,2,1,0:T(8,128)(2,1)} %bitcast.99, bf16[16,8,2,128,128]{4,3,2,1,0:T(8,128)(2,1)} %bitcast.92, pred[16,8]{1,0:T(8,128)(4,1)S(1)} %copy.45), kind=kOutput, calls=%fused_computation.13 | convolution fusion | flops 1078984704 | bytes 19923072 | tf_op jit(solution)/shard_map/dot_general | solution.py:72
  107.8 2.0 %collective-permute-start.8 = (bf16[2,128,1,128]{1,3,2,0:T(8,128)(2,1)S(1)}, bf16[2,128,1,128]{1,3,2,0:T(8,128)(2,1)S(1)}, u32[]{:S(2)}, u32[]{:S(2)}) collective-permute-start(bf16[2,128,1,128]{1,3,2,0:T(8,128)(2,1)S(1)} %get-tuple-element.20), channel_id=1, source_target_pairs={{0,4},{4,8},{8,12},{1,5},{5,9},{9,13},{2,6},{6,10},{10,14},{3,7},{... | collective-permute-start | bytes 196616 | tf_op jit(solution)/shard_map/ppermute | solution.py:17
  109.8 1.3 collective-permute-start.9
  111.9 4.1 %collective-permute-done.9 = bf16[2,128,1,128]{1,3,2,0:T(8,128)(2,1)S(1)} collective-permute-done((bf16[2,128,1,128]{1,3,2,0:T(8,128)(2,1)S(1)}, bf16[2,128,1,128]{1,3,2,0:T(8,128)(2,1)S(1)}, u32[]{:S(2)}, u32[]{:S(2)}) %collective-permute-start.9) | collective-permute-done | bytes 65568 | tf_op jit(solution)/shard_map/ppermute | solution.py:18
  116.1 1.5 %collective-permute-start.10 = (bf16[2,128,18,1]{1,3,2,0:T(2,128)(2,1)S(1)}, bf16[2,128,18,1]{1,3,2,0:T(2,128)(2,1)S(1)}, u32[]{:S(2)}, u32[]{:S(2)}) collective-permute-start(bf16[2,128,18,1]{1,3,2,0:T(2,128)(2,1)S(1)} %get-tuple-element.18), channel_id=1, source_target_pairs={{0,1},{1,2},{2,3},{4,5},{5,6},{6,7},{8,9},{9,10},{10,11},{12,13},{... | collective-permute-start | bytes 27656 | tf_op jit(solution)/shard_map/ppermute | solution.py:17
  118.9 3.1 %convolution_convert_fusion = bf16[1024,128]{1,0:T(8,128)(2,1)} fusion(bf16[1024,4096]{0,1:T(8,128)(2,1)S(1)} %bitcast.85, bf16[128,4096]{0,1:T(8,128)(2,1)S(1)} %bitcast.91), kind=kOutput, calls=%fused_computation.26 | convolution fusion | flops 1073872896 | bytes 9699328 | tf_op jit(solution)/shard_map/dot_general | solution.py:124
  122.0 6.2 %all-to-all-start.3 = ((bf16[16,64,128]{2,1,0:T(8,128)(2,1)}), bf16[16,64,128]{2,1,0:T(8,128)(2,1)S(1)}, u32[]{:S(2)}, u32[]{:S(2)}) async-start(bf16[16,64,128]{2,1,0:T(8,128)(2,1)} %bitcast.36), calls=%async_computation.3 | async-start | bytes 524288 | tf_op jit(solution)/shard_map/all_to_all | solution.py:127
  129.3 1.4 copy.59
  130.6 7.6 %all-to-all-done.3 = bf16[16,64,128]{2,1,0:T(8,128)(2,1)S(1)} async-done(((bf16[16,64,128]{2,1,0:T(8,128)(2,1)}), bf16[16,64,128]{2,1,0:T(8,128)(2,1)S(1)}, u32[]{:S(2)}, u32[]{:S(2)}) %all-to-all-start.3) | async-done | bytes 262176 | tf_op jit(solution)/shard_map/all_to_all | solution.py:127
  138.2 1.4 %fusion.17 = bf16[512,128]{1,0:T(8,128)(2,1)} fusion(bf16[1024,128]{1,0:T(8,128)(2,1)S(1)} %bitcast.97, s32[512]{0:T(512)S(1)} %multiply_add_fusion), kind=kOutput, calls=%fused_computation.27 | convolution fusion | flops 134807552 | bytes 395264 | tf_op jit(solution)/shard_map/dot_general | solution.py:135
  (67 shorter events, 16.6 us)
Async XLA Ops:
  0.6 19.2 %copy-start = (bf16[512,128]{1,0:T(8,128)(2,1)S(1)}, bf16[512,128]{1,0:T(8,128)(2,1)}, u32[]{:S(2)}) copy-start(bf16[512,128]{1,0:T(8,128)(2,1)} %param.10) | copy-start | bytes 393220
  2.6 15.9 %copy-start.4 = (bf16[512,2,128]{2,1,0:T(2,128)(2,1)S(1)}, bf16[512,2,128]{2,1,0:T(2,128)(2,1)}, u32[]{:S(2)}) copy-start(bf16[512,2,128]{2,1,0:T(2,128)(2,1)} %param.11) | copy-start | bytes 786436
  4.0 36.5 %all-to-all-start.1 = ((s32[16,1,64]{2,1,0:T(1,128)}), s32[16,1,64]{2,1,0:T(1,128)S(1)}, u32[]{:S(2)}, u32[]{:S(2)}) async-start(s32[16,1,64]{2,1,0:T(1,128)} %all_to_all.16), calls=%async_computation.1 | async-start | bytes 16384 | tf_op jit(solution)/shard_map/all_to_all | solution.py:106
  13.3 7.7 %collective-permute-start = (f32[128,1,256]{0,2,1:T(8,128)S(1)}, f32[128,1,256]{0,2,1:T(8,128)S(1)}, u32[]{:S(2)}, u32[]{:S(2)}) collective-permute-start(f32[128,1,256]{0,2,1:T(8,128)S(1)} %get-tuple-element.12), channel_id=1, source_target_pairs={{0,4},{4,8},{8,12},{1,5},{5,9},{9,13},{2,6},{6,10},{10,14},{3,7},{... | collective-permute-start | bytes 393224 | tf_op jit(solution)/shard_map/ppermute | solution.py:17
  17.2 7.2 %collective-permute-start.1 = (f32[128,1,256]{0,2,1:T(8,128)S(1)}, f32[128,1,256]{0,2,1:T(8,128)S(1)}, u32[]{:S(2)}, u32[]{:S(2)}) collective-permute-start(f32[128,1,256]{0,2,1:T(8,128)S(1)} %get-tuple-element.13), channel_id=1, source_target_pairs={{4,0},{8,4},{12,8},{5,1},{9,5},{13,9},{6,2},{10,6},{14,10},{7,3},{... | collective-permute-start | bytes 393224 | tf_op jit(solution)/shard_map/ppermute | solution.py:18
  18.5 11.7 %copy-start.3 = (s32[2,8,8]{2,1,0:T(8,128)S(1)}, s32[2,8,8]{2,1,0:T(8,128)}, u32[]{:S(2)}) copy-start(s32[2,8,8]{2,1,0:T(8,128)} %param.8) | copy-start | bytes 1540
  24.4 5.9 %collective-permute-start.3 = (f32[128,18,1]{0,2,1:T(1,128)S(1)}, f32[128,18,1]{0,2,1:T(1,128)S(1)}, u32[]{:S(2)}, u32[]{:S(2)}) collective-permute-start(f32[128,18,1]{0,2,1:T(1,128)S(1)} %get-tuple-element.8), channel_id=1, source_target_pairs={{2,0},{3,1},{6,4},{7,5},{10,8},{11,9},{14,12},{15,13},{18,16},{19,... | collective-permute-start | bytes 27656 | tf_op jit(solution)/shard_map/ppermute | solution.py:18
  25.7 5.9 %collective-permute-start.2 = (f32[128,18,1]{0,2,1:T(1,128)S(1)}, f32[128,18,1]{0,2,1:T(1,128)S(1)}, u32[]{:S(2)}, u32[]{:S(2)}) collective-permute-start(f32[128,18,1]{0,2,1:T(1,128)S(1)} %get-tuple-element.9), channel_id=1, source_target_pairs={{0,2},{1,3},{4,6},{5,7},{8,10},{9,11},{12,14},{13,15},{16,18},{17,... | collective-permute-start | bytes 27656 | tf_op jit(solution)/shard_map/ppermute | solution.py:17
  34.4 13.8 %collective-permute-start.5 = (bf16[1,8,2,128,128]{3,4,2,1,0:T(8,128)(2,1)}, bf16[1,8,2,128,128]{3,4,2,1,0:T(8,128)(2,1)S(1)}, u32[]{:S(2)}, u32[]{:S(2)}) collective-permute-start(bf16[1,8,2,128,128]{3,4,2,1,0:T(8,128)(2,1)} %bitcast.6), channel_id=1, source_target_pairs={{4,0},{8,4},{12,8},{5,1},{9,5},{13,9},{6,2},{10,6},{14,10},{7,3},{... | collective-permute-start | bytes 1572872 | tf_op jit(solution)/shard_map/ppermute | solution.py:18
  35.7 16.1 %collective-permute-start.4 = (bf16[1,8,2,128,128]{3,4,2,1,0:T(8,128)(2,1)}, bf16[1,8,2,128,128]{3,4,2,1,0:T(8,128)(2,1)S(1)}, u32[]{:S(2)}, u32[]{:S(2)}) collective-permute-start(bf16[1,8,2,128,128]{3,4,2,1,0:T(8,128)(2,1)} %bitcast.4), channel_id=1, source_target_pairs={{0,4},{4,8},{8,12},{1,5},{5,9},{9,13},{2,6},{6,10},{10,14},{3,7},{... | collective-permute-start | bytes 1572872 | tf_op jit(solution)/shard_map/ppermute | solution.py:17
  40.5 30.1 %all-to-all-start.2 = ((bf16[16,64,256]{2,1,0:T(8,128)(2,1)}), bf16[16,64,256]{2,1,0:T(8,128)(2,1)}, u32[]{:S(2)}, u32[]{:S(2)}) async-start(bf16[16,64,256]{2,1,0:T(8,128)(2,1)} %bitcast.19), calls=%async_computation.2 | async-start | bytes 1048576 | tf_op jit(solution)/shard_map/all_to_all | solution.py:104
  46.3 12.7 %copy-start.1 = (bf16[2,8,2,128,8,16]{3,5,4,2,1,0:T(8,128)(2,1)}, bf16[2,8,2,128,8,16]{3,5,4,2,1,0:T(8,128)(2,1)S(1)}, u32[]{:S(2)}) copy-start(bf16[2,8,2,128,8,16]{3,5,4,2,1,0:T(8,128)(2,1)S(1)} %copy.50) | copy-start | bytes 3145732
  51.8 4.0 %collective-permute-start.6 = (bf16[4,1,2,128,128]{3,4,2,1,0:T(8,128)(2,1)S(1)}, bf16[4,1,2,128,128]{3,4,2,1,0:T(8,128)(2,1)S(1)}, u32[]{:S(2)}, u32[]{:S(2)}) collective-permute-start(bf16[4,1,2,128,128]{3,4,2,1,0:T(8,128)(2,1)S(1)} %get-tuple-element.10), channel_id=1, source_target_pairs={{0,1},{1,2},{2,3},{4,5},{5,6},{6,7},{8,9},{9,10},{10,11},{12,13},{... | collective-permute-start | bytes 786440 | tf_op jit(solution)/shard_map/ppermute | solution.py:17
  53.1 6.0 %collective-permute-start.7 = (bf16[4,1,2,128,128]{3,4,2,1,0:T(8,128)(2,1)S(1)}, bf16[4,1,2,128,128]{3,4,2,1,0:T(8,128)(2,1)S(1)}, u32[]{:S(2)}, u32[]{:S(2)}) collective-permute-start(bf16[4,1,2,128,128]{3,4,2,1,0:T(8,128)(2,1)S(1)} %get-tuple-element.11), channel_id=1, source_target_pairs={{1,0},{2,1},{3,2},{5,4},{6,5},{7,6},{9,8},{10,9},{11,10},{13,12},{... | collective-permute-start | bytes 786440 | tf_op jit(solution)/shard_map/ppermute | solution.py:18
  70.6 23.3 %all-to-all-start = ((bf16[16,64,128]{2,1,0:T(8,128)(2,1)}), bf16[16,64,128]{2,1,0:T(8,128)(2,1)S(1)}, u32[]{:S(2)}, u32[]{:S(2)}) async-start(bf16[16,64,128]{2,1,0:T(8,128)(2,1)} %bitcast.15), calls=%async_computation | async-start | bytes 524288 | tf_op jit(solution)/shard_map/all_to_all | solution.py:105
  93.9 24.9 %slice-start = ((s8[8388608]{0:T(1024)(128)(4,1)}), s8[4194304]{0:T(1024)(128)(4,1)S(1)}, s32[]{:S(2)}) async-start(s8[8388608]{0:T(1024)(128)(4,1)} %bitcast.83), calls=%async_computation.4 | async-start | bytes 8388608
  99.8 19.1 %slice-start.1 = ((s8[8388608]{0:T(1024)(128)(4,1)}), s8[4194304]{0:T(1024)(128)(4,1)S(1)}, s32[]{:S(2)}) async-start(s8[8388608]{0:T(1024)(128)(4,1)} %bitcast.83), calls=%async_computation.5 | async-start | bytes 8388608
  107.5 11.4 %copy-start.2 = (bf16[2,8,2,128,8,16]{3,5,4,2,1,0:T(8,128)(2,1)S(1)}, bf16[2,8,2,128,8,16]{3,5,4,2,1,0:T(8,128)(2,1)}, u32[]{:S(2)}) copy-start(bf16[2,8,2,128,8,16]{3,5,4,2,1,0:T(8,128)(2,1)} %copy-done.1) | copy-start | bytes 3145732
  107.8 4.1 %collective-permute-start.8 = (bf16[2,128,1,128]{1,3,2,0:T(8,128)(2,1)S(1)}, bf16[2,128,1,128]{1,3,2,0:T(8,128)(2,1)S(1)}, u32[]{:S(2)}, u32[]{:S(2)}) collective-permute-start(bf16[2,128,1,128]{1,3,2,0:T(8,128)(2,1)S(1)} %get-tuple-element.20), channel_id=1, source_target_pairs={{0,4},{4,8},{8,12},{1,5},{5,9},{9,13},{2,6},{6,10},{10,14},{3,7},{... | collective-permute-start | bytes 196616 | tf_op jit(solution)/shard_map/ppermute | solution.py:17
  109.8 6.3 %collective-permute-start.9 = (bf16[2,128,1,128]{1,3,2,0:T(8,128)(2,1)S(1)}, bf16[2,128,1,128]{1,3,2,0:T(8,128)(2,1)S(1)}, u32[]{:S(2)}, u32[]{:S(2)}) collective-permute-start(bf16[2,128,1,128]{1,3,2,0:T(8,128)(2,1)S(1)} %get-tuple-element.21), channel_id=1, source_target_pairs={{4,0},{8,4},{12,8},{5,1},{9,5},{13,9},{6,2},{10,6},{14,10},{7,3},{... | collective-permute-start | bytes 196616 | tf_op jit(solution)/shard_map/ppermute | solution.py:18
  116.1 12.1 %collective-permute-start.10 = (bf16[2,128,18,1]{1,3,2,0:T(2,128)(2,1)S(1)}, bf16[2,128,18,1]{1,3,2,0:T(2,128)(2,1)S(1)}, u32[]{:S(2)}, u32[]{:S(2)}) collective-permute-start(bf16[2,128,18,1]{1,3,2,0:T(2,128)(2,1)S(1)} %get-tuple-element.18), channel_id=1, source_target_pairs={{0,1},{1,2},{2,3},{4,5},{5,6},{6,7},{8,9},{9,10},{10,11},{12,13},{... | collective-permute-start | bytes 27656 | tf_op jit(solution)/shard_map/ppermute | solution.py:17
  117.6 10.6 %collective-permute-start.11 = (bf16[2,128,18,1]{1,3,2,0:T(2,128)(2,1)S(1)}, bf16[2,128,18,1]{1,3,2,0:T(2,128)(2,1)S(1)}, u32[]{:S(2)}, u32[]{:S(2)}) collective-permute-start(bf16[2,128,18,1]{1,3,2,0:T(2,128)(2,1)S(1)} %get-tuple-element.19), channel_id=1, source_target_pairs={{1,0},{2,1},{3,2},{5,4},{6,5},{7,6},{9,8},{10,9},{11,10},{13,12},{... | collective-permute-start | bytes 27656 | tf_op jit(solution)/shard_map/ppermute | solution.py:18
  122.0 16.3 %all-to-all-start.3 = ((bf16[16,64,128]{2,1,0:T(8,128)(2,1)}), bf16[16,64,128]{2,1,0:T(8,128)(2,1)S(1)}, u32[]{:S(2)}, u32[]{:S(2)}) async-start(bf16[16,64,128]{2,1,0:T(8,128)(2,1)} %bitcast.36), calls=%async_computation.3 | async-start | bytes 524288 | tf_op jit(solution)/shard_map/all_to_all | solution.py:127
where the time goes:
time: 141 us; the launch traced here: 140 us
  starting transfers between devices  57.8 us (41%)
  waiting for transfers between devices  30.7 us (22%)
  matrix products  20.6 us (15%)
  local copies, waits for them, and re-layouts  18.7 us (13%)
  other arithmetic  10.8 us (8%)
    ppermute x6, starting transfers between devices, with_halo(): before = lax.ppermute(last, axis, up)  17.7 us
    all_to_all x1, starting transfers between devices, body(): lax.all_to_all(send_current, ('gx', 'gy', 'gz'), split_axis=0, concat_axi...  13.3 us
    ppermute x6, waiting for transfers between devices, with_halo(): after = lax.ppermute(leading, axis, down)  12.5 us
    ppermute x6, starting transfers between devices, with_halo(): after = lax.ppermute(leading, axis, down)  7.74 us
    dot_general x1, matrix products, body(): lax.dot_general(sources, kernels, (((1, 4), (1, 4)), ((0, 2), (0, 2))), p...  7.68 us
    all_to_all x1, waiting for transfers between devices, body(): lax.all_to_all(induced.reshape(owners, capacity, port_count), ('gx', 'gy'...  7.61 us
    all_to_all x1, starting transfers between devices, body(): lax.all_to_all(send_leaf, ('gx', 'gy', 'gz'), split_axis=0, concat_axis=0...  7.36 us
    gather x1, local copies, waits for them, and re-layouts, body(): jnp.take(flattened, source.reshape(-1), axis=0)  6.56 us
  transfers between devices with their start and end apart: 16, of which 9 were waited for; matrix products, arithmetic and copies ran while one was open for 23% of the time, Pallas kernels for 0%

commit v1 on v0

v1 whole, which is shorter than its diff:
```python
import functools

import jax
import jax.numpy as jnp
from jax import lax
from jax.experimental import pallas as pl
from jax.experimental.pallas import tpu as pltpu
from jax.sharding import PartitionSpec as P

LEAF_R = 8
LEAF_C = 16
LANES = 128
BF = jnp.bfloat16
F32 = jnp.float32


def edges(value, axes, dim):
    size, length = lax.axis_size(axes), value.shape[dim]
    up = [(i, i + 1) for i in range(size - 1)]
    down = [(j, i) for i, j in up]
    last = lax.index_in_dim(value, length - 1, axis=dim, keepdims=False)
    first = lax.index_in_dim(value, 0, axis=dim, keepdims=False)
    before = lax.ppermute(last, axes, up)
    after = lax.ppermute(first, axes, down)
    return jnp.expand_dims(before, dim), jnp.expand_dims(after, dim)


def to_leaves(grid_values):
    components, port_count, row_count, col_count = grid_values.shape
    blocks = grid_values.reshape(
        components, port_count, row_count // LEAF_R, LEAF_R, col_count // LEAF_C, LEAF_C
    )
    blocks = blocks.transpose(2, 4, 0, 1, 3, 5)
    return blocks.reshape(
        row_count // LEAF_R, col_count // LEAF_C, components, port_count, LEAF_R * LEAF_C
    )


def from_leaves(leaves):
    leaf_rows, leaf_cols, components, port_count, leaf_cells = leaves.shape
    blocks = leaves.reshape(leaf_rows, leaf_cols, components, port_count, LEAF_R, LEAF_C)
    blocks = blocks.transpose(2, 3, 0, 4, 1, 5)
    return blocks.reshape(components, port_count, leaf_rows * LEAF_R, leaf_cols * LEAF_C)


def kernel(
    dims, near_ref, leaves_ref, send_ref, ids_ref, ind_hbm, field_ref, ret_ref,
    bordered, got, got_ids, ind, near_acc, volt, ret_send, current_t,
    ind_sem, halo_send, halo_recv, block_send, block_recv, id_send, id_recv, ret_ssem, ret_rsem,
):
    nx, ny, nz = dims
    nyz = ny * nz
    owners = nx * nyz
    leaf_rows, leaf_cols = leaves_ref.shape[:2]
    near_count = ind.shape[1]
    cap = send_ref.shape[1]
    slots = owners * cap
    mx, my, mz = lax.axis_index("gx"), lax.axis_index("gy"), lax.axis_index("gz")
    mc = my * nz + mz
    me = mx * nyz + mc

    def device(x, c):
        return {"gx": x, "gy": c // nz, "gz": c % nz}

    def peer(d):
        return device(d // nyz, d % nyz)

    ind_copy = pltpu.make_async_copy(ind_hbm, ind, ind_sem)
    ind_copy.start()
    barrier = pltpu.get_barrier_semaphore()

    @pl.loop(1, owners)
    def _(k):
        pl.semaphore_signal(
            barrier, inc=1, device_id=peer((me + k) % owners), device_id_type=pl.DeviceIdType.MESH
        )

    for r in range(leaf_rows):
        for j in range(leaf_cols):
            bordered[r + 1, j + 1] = leaves_ref[r, j]

    near_mesh = pl.DeviceIdType.MESH
    row_in = pl.ds(0, leaf_rows)
    row_at = pl.ds(1, leaf_rows)
    col_in = pl.ds(0, leaf_cols)
    col_at = pl.ds(1, leaf_cols)
    one = pl.ds(0, 1)
    plans = []
    for dx in (-1, 0, 1):
        for dc in (-1, 0, 1):
            if dx == 0 and dc == 0:
                continue
            src_r = row_in if dx == 0 else pl.ds(0 if dx < 0 else leaf_rows - 1, 1)
            dst_r = row_at if dx == 0 else pl.ds(leaf_rows + 1 if dx < 0 else 0, 1)
            src_c = col_in if dc == 0 else pl.ds(0 if dc < 0 else leaf_cols - 1, 1)
            dst_c = col_at if dc == 0 else pl.ds(leaf_cols + 1 if dc < 0 else 0, 1)
            plans.append((dx, dc, src_r, src_c, dst_r, dst_c))

    def halo(number):
        dx, dc, src_r, src_c, dst_r, dst_c = plans[number]
        return pltpu.make_async_remote_copy(
            src_ref=leaves_ref.at[src_r, src_c],
            dst_ref=bordered.at[dst_r, dst_c],
            send_sem=halo_send.at[number],
            recv_sem=halo_recv.at[number],
            device_id=device(mx + dx, mc + dc),
            device_id_type=near_mesh,
        )

    def inside(dx, dc):
        x, c = mx + dx, mc + dc
        return (x >= 0) & (x < nx) & (c >= 0) & (c < nyz)

    for number, (dx, dc, _, _, dst_r, dst_c) in enumerate(plans):
        @pl.when(jnp.logical_not(inside(-dx, -dc)))
        def _():
            view = bordered.at[dst_r, dst_c]
            view[...] = jnp.zeros(view.shape, BF)

    pl.semaphore_wait(barrier, owners - 1)

    for number, (dx, dc, _, _, _, _) in enumerate(plans):
        @pl.when(inside(dx, dc))
        def _():
            halo(number).start()

    def exchange(src, dst, ssem, rsem, d, slot):
        return pltpu.make_async_remote_copy(
            src_ref=src.at[d], dst_ref=dst.at[slot], send_sem=ssem.at[d], recv_sem=rsem.at[slot],
            device_id=peer(d), device_id_type=near_mesh,
        )

    @pl.loop(1, owners)
    def _(k):
        d = (me + k) % owners
        exchange(ids_ref, got_ids, id_send, id_recv, d, me).start()
        exchange(send_ref, got, block_send, block_recv, d, me).start()

    got[me] = send_ref[me]
    got_ids[me] = ids_ref[me]

    for number, (dx, dc, _, _, _, _) in enumerate(plans):
        @pl.when(inside(-dx, -dc))
        def _():
            halo(number).wait_recv()

    ind_copy.wait()

    @pl.loop(0, leaf_rows * leaf_cols)
    def _(l):
        for c in range(2):
            sources = jnp.concatenate(
                [bordered[near_ref[0, l * near_count + n], near_ref[1, l * near_count + n], c]
                 for n in range(near_count)], axis=1)
            tiles = jnp.concatenate([ind[l, n, c] for n in range(near_count)], axis=1)
            near_acc[l, :, c * LANES:(c + 1) * LANES] = lax.dot_general(
                sources, tiles, (((1,), (1,)), ((), ())), preferred_element_type=F32)

    @pl.loop(1, owners)
    def _(k):
        s = (me + k) % owners
        exchange(ids_ref, got_ids, id_send, id_recv, s, s).wait_recv()
        exchange(send_ref, got, block_send, block_recv, s, s).wait_recv()

    per_row = LANES // cap
    rows = []
    for g in range(slots // LANES):
        total = got_ids[g * per_row]
        for o in range(1, per_row):
            total = total + got_ids[g * per_row + o]
        rows.append(total)
    ids_row = jnp.concatenate(rows, axis=1) - 1.0
    coupling = got[:, :, : 2 * LANES].reshape(slots, 2 * LANES)
    current_t[...] = got[:, :, 2 * LANES:].reshape(slots, LANES).astype(F32).T.astype(BF)
    volt[...] = jnp.zeros_like(volt)

    @pl.loop(0, leaf_rows * leaf_cols)
    def _(l):
        hit = ids_row == l.astype(F32)
        plane = jnp.concatenate(
            [leaves_ref[l // leaf_cols, l % leaf_cols, c] for c in range(2)], axis=1)
        part = lax.dot_general(
            plane, coupling, (((1,), (1,)), ((), ())), preferred_element_type=F32)
        volt[...] += jnp.where(hit, part, 0.0)

    ret_send[...] = volt[...].T.astype(BF).reshape(owners, cap, LANES)

    @pl.loop(1, owners)
    def _(k):
        d = (me + k) % owners
        exchange(ret_send, ret_ref, ret_ssem, ret_rsem, d, me).start()

    ret_ref[me] = ret_send[me]

    @pl.loop(0, leaf_rows * leaf_cols)
    def _(l):
        hit = ids_row == l.astype(F32)
        masked = jnp.where(hit, current_t[...], jnp.zeros((), BF))
        part = near_acc[l] + jnp.dot(masked, coupling, preferred_element_type=F32)
        for c in range(2):
            field_ref[l, c] = part[:, c * LANES:(c + 1) * LANES].astype(BF)

    @pl.loop(1, owners)
    def _(k):
        s = (me + k) % owners
        exchange(ids_ref, got_ids, id_send, id_recv, s, s).wait_send()
        exchange(send_ref, got, block_send, block_recv, s, s).wait_send()
        exchange(ret_send, ret_ref, ret_ssem, ret_rsem, s, s).wait()

    for number, (dx, dc, _, _, _, _) in enumerate(plans):
        @pl.when(inside(dx, dc))
        def _():
            halo(number).wait_send()


def body(stream, inductance, near_lists, filament_leaf, filament_current, filament_coupling):
    port_count = stream.shape[0]
    leaf_rows, leaf_cols, near_count, _, leaf_cells, _ = inductance.shape
    leaf_count = leaf_rows * leaf_cols
    half_cols = leaf_cols * LEAF_C
    nx, ny, nz = lax.axis_size("gx"), lax.axis_size("gy"), lax.axis_size("gz")
    owners = nx * ny * nz
    first_col = lax.axis_index("gz") * half_cols
    me = (lax.axis_index("gx") * ny + lax.axis_index("gy")) * nz + lax.axis_index("gz")

    left, right = edges(stream, "gy", 2)
    above, below = edges(stream, "gx", 1)
    wide = jnp.concatenate([left, stream, right], axis=2)
    window = lax.dynamic_slice_in_dim(wide, first_col, half_cols + 2, 2)
    tall = lax.dynamic_slice_in_dim(
        jnp.concatenate([above, stream, below], axis=1), first_col, half_cols, 2)
    currents = jnp.stack([window[:, :, 2:] - window[:, :, :-2], tall[:, :-2] - tall[:, 2:]]).astype(BF)
    leaves = to_leaves(currents)

    row_index = jnp.arange(leaf_rows, dtype=jnp.int32)[:, None, None] + near_lists // 3
    col_index = jnp.arange(leaf_cols, dtype=jnp.int32)[None, :, None] + near_lists % 3
    near_index = jnp.stack([row_index.reshape(-1), col_index.reshape(-1)])

    filament_count = filament_leaf.shape[0]
    capacity = max(16, 2 * filament_count // owners)
    slot_count = owners * capacity
    plane_cols = leaf_cols * ny * nz
    leaf_row = filament_leaf // plane_cols
    leaf_col = filament_leaf % plane_cols
    owner_ids = leaf_row // leaf_rows * (ny * nz) + leaf_col // leaf_cols
    local_ids = leaf_row % leaf_rows * leaf_cols + leaf_col % leaf_cols
    owner_hits = owner_ids[:, None] == jnp.arange(owners, dtype=jnp.int32)[None, :]
    numbers = jnp.arange(filament_count, dtype=jnp.int32)
    earlier = (numbers[None, :] < numbers[:, None]).astype(BF)
    ranks = jnp.dot(earlier, owner_hits.astype(BF), preferred_element_type=F32)
    position = jnp.sum(jnp.where(owner_hits, ranks, 0.0), axis=1).astype(jnp.int32)
    target_slot = owner_ids * capacity + position
    placement_mask = target_slot[None, :] == jnp.arange(slot_count, dtype=jnp.int32)[:, None]
    placement = placement_mask.astype(BF)
    rows = jnp.concatenate(
        [filament_coupling.reshape(filament_count, 2 * leaf_cells), filament_current], axis=1)
    send = jnp.dot(placement, rows, preferred_element_type=F32).astype(BF)
    send = send.reshape(owners, capacity, 2 * leaf_cells + port_count)
    sent_leaf = jnp.max(jnp.where(placement_mask, local_ids[None, :] + 1, 0), axis=1).astype(F32)
    per_row = LANES // capacity
    lane_part = (jnp.arange(per_row, dtype=jnp.int32) == me % per_row).astype(F32)
    ids = (sent_leaf.reshape(owners, 1, capacity) * lane_part[None, :, None]).reshape(owners, 1, LANES)

    vmem = pl.BlockSpec(memory_space=pltpu.VMEM)
    dma = pltpu.SemaphoreType.DMA
    field, returned = pl.pallas_call(
        functools.partial(kernel, (nx, ny, nz)),
        out_shape=(
            jax.ShapeDtypeStruct((leaf_count, 2, port_count, leaf_cells), BF),
            jax.ShapeDtypeStruct((owners, capacity, port_count), BF),
        ),
        in_specs=[pl.BlockSpec(memory_space=pltpu.SMEM), vmem, vmem, vmem,
                  pl.BlockSpec(memory_space=pl.ANY)],
        out_specs=(vmem, vmem),
        scratch_shapes=[
            pltpu.VMEM((leaf_rows + 2, leaf_cols + 2, 2, port_count, leaf_cells), BF),
            pltpu.VMEM(send.shape, BF),
            pltpu.VMEM(ids.shape, F32),
            pltpu.VMEM((leaf_count, near_count, 2, leaf_cells, leaf_cells), BF),
            pltpu.VMEM((leaf_count, port_count, 2 * leaf_cells), F32),
            pltpu.VMEM((port_count, slot_count), F32),
            pltpu.VMEM((owners, capacity, port_count), BF),
            pltpu.VMEM((port_count, slot_count), BF),
            dma, dma((8,)), dma((8,)),
            dma((owners,)), dma((owners,)), dma((owners,)), dma((owners,)),
            dma((owners,)), dma((owners,)),
        ],
        compiler_params=pltpu.CompilerParams(
            collective_id=0, has_side_effects=True, vmem_limit_bytes=40 * 2**20),
        cost_estimate=pl.CostEstimate(
            flops=3 * 2 * 2**29, bytes_accessed=12 * 2**20, transcendentals=0),
    )(near_index, leaves, send, ids,
      inductance.reshape(leaf_count, near_count, 2, leaf_cells, leaf_cells))

    filament_voltage = lax.dot_general(
        placement, returned.reshape(slot_count, port_count), (((0,), (0,)), ((), ())),
        preferred_element_type=F32).astype(BF)
    grid_field = from_leaves(field.reshape(leaf_rows, leaf_cols, 2, port_count, leaf_cells))
    x_field, y_field = grid_field[0], grid_field[1]
    left, right = edges(x_field, ("gy", "gz"), 2)
    above, below = edges(y_field, "gx", 1)
    x_wide = jnp.concatenate([left, x_field, right], axis=2).astype(F32)
    y_tall = jnp.concatenate([above, y_field, below], axis=1).astype(F32)
    loop_voltage = (x_wide[:, :, :-2] - x_wide[:, :, 2:]) + (y_tall[:, 2:] - y_tall[:, :-2])
    return (loop_voltage, filament_voltage)


def solution(mesh):
    return jax.shard_map(
        body,
        mesh=mesh,
        in_specs=(
            P("groups", "gx", "gy"),
            P(("groups", "gx"), ("gy", "gz"), None, None, None, None),
            P(("groups", "gx"), ("gy", "gz"), None),
            P(("groups", "gx", "gy", "gz")),
            P(("groups", "gx", "gy", "gz"), None),
            P(("groups", "gx", "gy", "gz"), None, None),
        ),
        out_specs=(P("groups", "gx", ("gy", "gz")), P(("groups", "gx", "gy", "gz"), None)),
        check_vma=False,
    )
```

time: 141 us -> 98.4 us (0.70)
  Pallas kernels: 0 us -> 50.4 us
  starting transfers between devices: 57.8 us -> 20.4 us
  waiting for transfers between devices: 30.7 us -> 3.26 us
  matrix products: 20.6 us -> 2.43 us
  other arithmetic: 10.8 us -> 2.41 us
  local copies, waits for them, and re-layouts: 18.7 us -> 17 us
    pallas_call x0 -> x1, Pallas kernels: none -> 50.4 us  [body(): pl.pallas_call(functools.partial(kernel, (nx, ny, nz)), out_shape=(jax.Sh...]
    all_to_all x4 -> x0, starting transfers between devices: 32.4 us -> none  [the longest x1 13.3 us: body(): lax.all_to_all(send_current, ('gx', 'gy', 'gz'), split_axis=0, concat_axi...]
    dot_general x6 -> x3, matrix products: 20.6 us -> 2.43 us  [the longest x1 1.44 us: body(): lax.dot_general(placement, returned.reshape(slot_count, port_count), (((0...]
    ppermute x12 -> x8, waiting for transfers between devices: 18.2 us -> 3.26 us  [the longest x4 3.25 us: edges(): after = lax.ppermute(first, axes, down)]
    all_to_all x4 -> x0, waiting for transfers between devices: 12.5 us -> none  [the longest x1 7.61 us: body(): lax.all_to_all(induced.reshape(owners, capacity, port_count), ('gx', 'gy'...]
    gather x1 -> x0, local copies, waits for them, and re-layouts: 6.56 us -> none  [body(): jnp.take(flattened, source.reshape(-1), axis=0)]
    ppermute x12 -> x8, starting transfers between devices: 25.4 us -> 20.4 us  [the longest x4 15.1 us: edges(): before = lax.ppermute(last, axes, up)]
    unnamed x16 -> x19, local copies, waits for them, and re-layouts: 3.41 us -> 8.36 us
  transfers between devices with their start and end apart: 16 -> 8, of which waited for: 9 -> 2; matrix products, arithmetic and copies ran while one was open for 23% -> 10% of each run, Pallas kernels for 0% -> 0%
where the time goes in v1:
time: 98.4 us; the launch traced here: 96.9 us
  Pallas kernels  50.4 us (51%)
  starting transfers between devices  20.4 us (21%)
  local copies, waits for them, and re-layouts  17 us (17%)
  waiting for transfers between devices  3.26 us (3%)
  matrix products  2.43 us (2%)
  other arithmetic  2.41 us (2%)
  between operations  1.03 us (1%)
    pallas_call x1, Pallas kernels, body(): pl.pallas_call(functools.partial(kernel, (nx, ny, nz)), out_shape=(jax.Sh...  50.4 us
    ppermute x4, starting transfers between devices, edges(): before = lax.ppermute(last, axes, up)  15.1 us
    unnamed x19, local copies, waits for them, and re-layouts  8.36 us
    ppermute x4, starting transfers between devices, edges(): after = lax.ppermute(first, axes, down)  5.28 us
    slice x2, local copies, waits for them, and re-layouts, edges(): first = lax.index_in_dim(value, 0, axis=dim, keepdims=False)  3.61 us
    ppermute x4, waiting for transfers between devices, edges(): after = lax.ppermute(first, axes, down)  3.25 us
    broadcast_in_dim x4, local copies, waits for them, and re-layouts, edges(): return (jnp.expand_dims(before, dim), jnp.expand_dims(after, dim))  2.67 us
  transfers between devices with their start and end apart: 8, of which 2 were waited for; matrix products, arithmetic and copies ran while one was open for 10% of the time, Pallas kernels for 0%

profile of v1, /device:TPU:0, one launch (start us, length us, event | category | flops | bytes accessed | tf_op | source)
XLA Modules:
  0.0 96.9 jit_solution(8988895311777722082)
XLA Ops:
  0.6 1.9 %fusion.30 = (f32[128,16,1]{2,1,0:T(8,128)S(1)}, f32[128,16,1]{2,1,0:T(8,128)S(1)}) fusion(f32[128,16,256]{2,1,0:T(8,128)} %param.6), kind=kLoop, calls=%fused_computation.84 | loop fusion | bytes 32768 | tf_op jit(solution)/shard_map/slice | solution.py:22
  2.5 0.4 copy.103
  3.0 5.0 %collective-permute-start = (f32[128,16]{0,1:T(8,128)S(1)}, f32[128,16]{0,1:T(8,128)S(1)}, u32[]{:S(2)}, u32[]{:S(2)}) collective-permute-start(f32[128,16]{0,1:T(8,128)S(1)} %bitcast.65), channel_id=1, source_target_pairs={{0,2},{1,3},{4,6},{5,7},{8,10},{9,11},{12,14},{13,15},{16,18},{17,... | collective-permute-start | bytes 24584 | tf_op jit(solution)/shard_map/ppermute | solution.py:23
  7.9 0.4 copy.104
  8.4 1.4 %collective-permute-start.1 = (f32[128,16]{0,1:T(8,128)S(1)}, f32[128,16]{0,1:T(8,128)S(1)}, u32[]{:S(2)}, u32[]{:S(2)}) collective-permute-start(f32[128,16]{0,1:T(8,128)S(1)} %bitcast.67), channel_id=1, source_target_pairs={{2,0},{3,1},{6,4},{7,5},{10,8},{11,9},{14,12},{15,13},{18,16},{19,... | collective-permute-start | bytes 24584 | tf_op jit(solution)/shard_map/ppermute | solution.py:24
  9.8 1.7 %fusion.31 = (f32[128,1,256]{2,1,0:T(1,128)S(1)}, f32[128,1,256]{2,1,0:T(1,128)S(1)}) fusion(f32[128,16,256]{2,1,0:T(8,128)} %param.6), kind=kLoop, calls=%fused_computation.85 | loop fusion | bytes 524288 | tf_op jit(solution)/shard_map/slice | solution.py:22
  11.6 4.1 %collective-permute-start.2 = (f32[128,256]{1,0:T(8,128)S(1)}, f32[128,256]{1,0:T(8,128)}, u32[]{:S(2)}, u32[]{:S(2)}) collective-permute-start(f32[128,256]{1,0:T(8,128)S(1)} %bitcast.61), channel_id=1, source_target_pairs={{0,4},{4,8},{8,12},{1,5},{5,9},{9,13},{2,6},{6,10},{10,14},{3,7},{... | collective-permute-start | bytes 393224 | tf_op jit(solution)/shard_map/ppermute | solution.py:23
  15.7 0.7 copy.114
  16.4 1.3 %collective-permute-start.3 = (f32[128,256]{1,0:T(8,128)}, f32[128,256]{1,0:T(8,128)}, u32[]{:S(2)}, u32[]{:S(2)}) collective-permute-start(f32[128,256]{1,0:T(8,128)} %bitcast.44), channel_id=1, source_target_pairs={{4,0},{8,4},{12,8},{5,1},{9,5},{13,9},{6,2},{10,6},{14,10},{7,3},{... | collective-permute-start | bytes 393224 | tf_op jit(solution)/shard_map/ppermute | solution.py:24
  17.9 0.3 fusion.8
  18.2 0.4 select_reduce_fusion
  19.0 0.7 fusion.2
  19.7 2.0 %copy.83 = f32[128,16,256]{0,2,1:T(8,128)S(1)} copy(f32[128,16,256]{2,1,0:T(8,128)} %param.6) | data formatting | bytes 4194304 | tf_op args[0]
  21.7 0.3 fusion.7
  22.2 1.0 %copy.87 = f32[128,1,256]{0,2,1:T(8,128)S(1)} copy(f32[128,1,256]{2,0,1:T(8,128)} %bitcast.8) | data formatting | bytes 262144 | tf_op jit(solution)/shard_map/broadcast_in_dim | solution.py:25
  23.2 0.3 collective-permute-done.3
  23.5 1.7 %copy.89 = f32[128,1,256]{0,2,1:T(8,128)} copy(f32[128,1,256]{2,0,1:T(8,128)} %bitcast.10) | data formatting | bytes 262144 | tf_op jit(solution)/shard_map/broadcast_in_dim | solution.py:25
  25.2 0.9 fusion.4
  26.4 0.3 copy.90
  26.6 0.7 copy.91.leaves_ref
  27.3 3.4 %copy-done = bf16[2,8,8,2,128,128]{5,4,3,2,1,0:T(8,128)(2,1)S(1)} copy-done((bf16[2,8,8,2,128,128]{5,4,3,2,1,0:T(8,128)(2,1)S(1)}, bf16[2,8,8,2,128,128]{5,4,3,2,1,0:T(8,128)(2,1)}, u32[]{:S(2)}) %copy-start) | copy-done | bytes 8388632
  30.7 50.4 %shard_map.77 = (bf16[16,2,128,128]{3,2,1,0:T(8,128)(2,1)S(1)}, bf16[16,64,128]{2,1,0:T(8,128)(2,1)S(1)}) custom-call(s32[2,128]{1,0:T(2,128)S(1)} %pad_add_fusion.near_ref, bf16[2,8,2,128,128]{4,3,2,1,0:T(8,128)(2,1)S(1)} %copy.91.leaves_ref, bf16[16,64,384]{2,1,0:T(8,128)(2,1)S(1)} %bitcast.49, f32[16,1,128]{2,1,0:T(1,128)S(1)} %broadcast_multiply_fusion.ids_ref, ...), custom_call_target="tpu_custom_call" | custom-call | flops 3221225472 | bytes 12582912 | tf_op jit(solution)/shard_map/pallas_call | solution.py:266
  81.1 0.7 copy.92
  81.8 0.2 fusion.32
  82.0 2.1 %collective-permute-start.4 = (bf16[128,16]{0,1:T(8,128)(2,1)S(1)}, bf16[128,16]{0,1:T(8,128)(2,1)S(1)}, u32[]{:S(2)}, u32[]{:S(2)}) collective-permute-start(bf16[128,16]{0,1:T(8,128)(2,1)S(1)} %bitcast.68), channel_id=1, source_target_pairs={{0,1},{1,2},{2,3},{4,5},{5,6},{6,7},{8,9},{9,10},{10,11},{12,13},{... | collective-permute-start | bytes 12296 | tf_op jit(solution)/shard_map/ppermute | solution.py:23
  84.1 1.3 %collective-permute-start.5 = (bf16[128,16]{0,1:T(8,128)(2,1)S(1)}, bf16[128,16]{0,1:T(8,128)(2,1)S(1)}, u32[]{:S(2)}, u32[]{:S(2)}) collective-permute-start(bf16[128,16]{0,1:T(8,128)(2,1)S(1)} %bitcast.70), channel_id=1, source_target_pairs={{1,0},{2,1},{3,2},{5,4},{6,5},{7,6},{9,8},{10,9},{11,10},{13,12},{... | collective-permute-start | bytes 12296 | tf_op jit(solution)/shard_map/ppermute | solution.py:24
  85.5 3.9 %collective-permute-start.6 = (bf16[128,128]{0,1:T(8,128)(2,1)S(1)}, bf16[128,128]{0,1:T(8,128)(2,1)S(1)}, u32[]{:S(2)}, u32[]{:S(2)}) collective-permute-start(bf16[128,128]{0,1:T(8,128)(2,1)S(1)} %get-tuple-element.22), channel_id=1, source_target_pairs={{0,4},{4,8},{8,12},{1,5},{5,9},{9,13},{2,6},{6,10},{10,14},{3,7},{... | collective-permute-start | bytes 98312 | tf_op jit(solution)/shard_map/ppermute | solution.py:23
  89.4 1.3 %collective-permute-start.7 = (bf16[128,128]{0,1:T(8,128)(2,1)S(1)}, bf16[128,128]{0,1:T(8,128)(2,1)S(1)}, u32[]{:S(2)}, u32[]{:S(2)}) collective-permute-start(bf16[128,128]{0,1:T(8,128)(2,1)S(1)} %get-tuple-element.23), channel_id=1, source_target_pairs={{4,0},{8,4},{12,8},{5,1},{9,5},{13,9},{6,2},{10,6},{14,10},{7,3},{... | collective-permute-start | bytes 98312 | tf_op jit(solution)/shard_map/ppermute | solution.py:24
  90.7 1.4 %fusion.5 = bf16[512,128]{1,0:T(8,128)(2,1)} fusion(bf16[1024,128]{1,0:T(8,128)(2,1)S(1)} %bitcast.50, s32[512]{0:T(512)S(1)} %convert_add_fusion), kind=kOutput, calls=%fused_computation.13 | convolution fusion | flops 134807552 | bytes 395264 | tf_op jit(solution)/shard_map/dot_general | solution.py:295
  92.4 2.9 %collective-permute-done.7 = bf16[128,128]{0,1:T(8,128)(2,1)S(1)} collective-permute-done((bf16[128,128]{0,1:T(8,128)(2,1)S(1)}, bf16[128,128]{0,1:T(8,128)(2,1)S(1)}, u32[]{:S(2)}, u32[]{:S(2)}) %collective-permute-start.7) | collective-permute-done | bytes 32800 | tf_op jit(solution)/shard_map/ppermute | solution.py:24
  95.4 0.2 fusion.9
  95.6 1.4 %copy.99 = f32[128,16,128]{2,1,0:T(8,128)} copy(f32[128,16,128]{0,2,1:T(8,128)S(1)} %fusion.9) | data formatting | bytes 2097152
  (44 shorter events, 1.4 us)
Async XLA Ops:
  3.0 14.9 %copy-start.3 = (s32[512]{0:T(512)S(1)}, s32[512]{0:T(512)}, u32[]{:S(2)}) copy-start(s32[512]{0:T(512)} %param.9) | copy-start | bytes 6148
  3.0 18.8 %collective-permute-start = (f32[128,16]{0,1:T(8,128)S(1)}, f32[128,16]{0,1:T(8,128)S(1)}, u32[]{:S(2)}, u32[]{:S(2)}) collective-permute-start(f32[128,16]{0,1:T(8,128)S(1)} %bitcast.65), channel_id=1, source_target_pairs={{0,2},{1,3},{4,6},{5,7},{8,10},{9,11},{12,14},{13,15},{16,18},{17,... | collective-permute-start | bytes 24584 | tf_op jit(solution)/shard_map/ppermute | solution.py:23
  7.9 10.8 %copy-start.1 = (bf16[512,2,128]{2,1,0:T(2,128)(2,1)S(1)}, bf16[512,2,128]{2,1,0:T(2,128)(2,1)}, u32[]{:S(2)}) copy-start(bf16[512,2,128]{2,1,0:T(2,128)(2,1)} %param.11) | copy-start | bytes 786436
  8.4 10.3 %copy-start.2 = (s32[2,8,8]{2,1,0:T(8,128)S(1)}, s32[2,8,8]{2,1,0:T(8,128)}, u32[]{:S(2)}) copy-start(s32[2,8,8]{2,1,0:T(8,128)} %param.8) | copy-start | bytes 1540
  8.4 10.6 %copy-start.4 = (bf16[512,128]{1,0:T(8,128)(2,1)S(1)}, bf16[512,128]{1,0:T(8,128)(2,1)}, u32[]{:S(2)}) copy-start(bf16[512,128]{1,0:T(8,128)(2,1)} %param.10) | copy-start | bytes 393220
  8.4 13.3 %collective-permute-start.1 = (f32[128,16]{0,1:T(8,128)S(1)}, f32[128,16]{0,1:T(8,128)S(1)}, u32[]{:S(2)}, u32[]{:S(2)}) collective-permute-start(f32[128,16]{0,1:T(8,128)S(1)} %bitcast.67), channel_id=1, source_target_pairs={{2,0},{3,1},{6,4},{7,5},{10,8},{11,9},{14,12},{15,13},{18,16},{19,... | collective-permute-start | bytes 24584 | tf_op jit(solution)/shard_map/ppermute | solution.py:24
  11.6 10.6 %collective-permute-start.2 = (f32[128,256]{1,0:T(8,128)S(1)}, f32[128,256]{1,0:T(8,128)}, u32[]{:S(2)}, u32[]{:S(2)}) collective-permute-start(f32[128,256]{1,0:T(8,128)S(1)} %bitcast.61), channel_id=1, source_target_pairs={{0,4},{4,8},{8,12},{1,5},{5,9},{9,13},{2,6},{6,10},{10,14},{3,7},{... | collective-permute-start | bytes 393224 | tf_op jit(solution)/shard_map/ppermute | solution.py:23
  16.4 7.2 %collective-permute-start.3 = (f32[128,256]{1,0:T(8,128)}, f32[128,256]{1,0:T(8,128)}, u32[]{:S(2)}, u32[]{:S(2)}) collective-permute-start(f32[128,256]{1,0:T(8,128)} %bitcast.44), channel_id=1, source_target_pairs={{4,0},{8,4},{12,8},{5,1},{9,5},{13,9},{6,2},{10,6},{14,10},{7,3},{... | collective-permute-start | bytes 393224 | tf_op jit(solution)/shard_map/ppermute | solution.py:24
  27.3 3.4 %copy-start = (bf16[2,8,8,2,128,128]{5,4,3,2,1,0:T(8,128)(2,1)S(1)}, bf16[2,8,8,2,128,128]{5,4,3,2,1,0:T(8,128)(2,1)}, u32[]{:S(2)}) copy-start(bf16[2,8,8,2,128,128]{5,4,3,2,1,0:T(8,128)(2,1)} %param.7) | copy-start | bytes 25165828
  82.0 10.1 %collective-permute-start.4 = (bf16[128,16]{0,1:T(8,128)(2,1)S(1)}, bf16[128,16]{0,1:T(8,128)(2,1)S(1)}, u32[]{:S(2)}, u32[]{:S(2)}) collective-permute-start(bf16[128,16]{0,1:T(8,128)(2,1)S(1)} %bitcast.68), channel_id=1, source_target_pairs={{0,1},{1,2},{2,3},{4,5},{5,6},{6,7},{8,9},{9,10},{10,11},{12,13},{... | collective-permute-start | bytes 12296 | tf_op jit(solution)/shard_map/ppermute | solution.py:23
  84.1 8.0 %collective-permute-start.5 = (bf16[128,16]{0,1:T(8,128)(2,1)S(1)}, bf16[128,16]{0,1:T(8,128)(2,1)S(1)}, u32[]{:S(2)}, u32[]{:S(2)}) collective-permute-start(bf16[128,16]{0,1:T(8,128)(2,1)S(1)} %bitcast.70), channel_id=1, source_target_pairs={{1,0},{2,1},{3,2},{5,4},{6,5},{7,6},{9,8},{10,9},{11,10},{13,12},{... | collective-permute-start | bytes 12296 | tf_op jit(solution)/shard_map/ppermute | solution.py:24
  85.5 6.8 %collective-permute-start.6 = (bf16[128,128]{0,1:T(8,128)(2,1)S(1)}, bf16[128,128]{0,1:T(8,128)(2,1)S(1)}, u32[]{:S(2)}, u32[]{:S(2)}) collective-permute-start(bf16[128,128]{0,1:T(8,128)(2,1)S(1)} %get-tuple-element.22), channel_id=1, source_target_pairs={{0,4},{4,8},{8,12},{1,5},{5,9},{9,13},{2,6},{6,10},{10,14},{3,7},{... | collective-permute-start | bytes 98312 | tf_op jit(solution)/shard_map/ppermute | solution.py:23
  89.4 5.8 %collective-permute-start.7 = (bf16[128,128]{0,1:T(8,128)(2,1)S(1)}, bf16[128,128]{0,1:T(8,128)(2,1)S(1)}, u32[]{:S(2)}, u32[]{:S(2)}) collective-permute-start(bf16[128,128]{0,1:T(8,128)(2,1)S(1)} %get-tuple-element.23), channel_id=1, source_target_pairs={{4,0},{8,4},{12,8},{5,1},{9,5},{13,9},{6,2},{10,6},{14,10},{7,3},{... | collective-permute-start | bytes 98312 | tf_op jit(solution)/shard_map/ppermute | solution.py:24

commit v2 on v1

v2 whole, which is shorter than its diff:
```python
import functools

import jax
import jax.numpy as jnp
from jax import lax
from jax.experimental import pallas as pl
from jax.experimental.pallas import tpu as pltpu
from jax.sharding import PartitionSpec as P

LEAF_R = 8
LEAF_C = 16
LANES = 128
BF = jnp.bfloat16
F32 = jnp.float32


def exchange_blocks(values):
    lane_block = lax.broadcasted_iota(jnp.int32, values[0].shape, 1) // LEAF_C
    values = list(values)
    for bit in (1, 2, 4):
        low = (lane_block & bit) == 0
        shift = bit * LEAF_C
        for r in range(LEAF_R):
            if r & bit:
                continue
            a, b = values[r], values[r | bit]
            values[r] = jnp.where(low, a, pltpu.roll(b, shift, 1))
            values[r | bit] = jnp.where(low, pltpu.roll(a, LANES - shift, 1), b)
    return values


def sides(mid, before, after):
    lane = lax.broadcasted_iota(jnp.int32, mid.shape, 1)
    left = jnp.where(lane == 0, before, pltpu.roll(mid, 1, 1))
    right = jnp.where(lane == LANES - 1, after, pltpu.roll(mid, LANES - 1, 1))
    return left, right


CHUNK = 32


def kernel(
    dims, near_ref, tile_ref, send_ref, ids_ref, ind_hbm, loop_ref, ret_ref,
    stream_ref, bordered, planes, got, got_ids, ind, acc, ret_send, grid,
    col_out, row_in, col_in, frow_out, fcol_out, frow_in, fcol_in,
    ind_sem, halo_send, halo_recv, edge_send, edge_recv, fedge_send, fedge_recv,
    block_send, block_recv, id_send, id_recv, ret_ssem, ret_rsem,
):
    nx, ny, nz = dims
    nyz = ny * nz
    owners = nx * nyz
    leaf_rows, leaf_cols = bordered.shape[0] - 2, bordered.shape[1] - 2
    leaf_count = leaf_rows * leaf_cols
    ports, row_count = tile_ref.shape[:2]
    near_count = ind.shape[1]
    cap = send_ref.shape[1]
    mx, my, mz = lax.axis_index("gx"), lax.axis_index("gy"), lax.axis_index("gz")
    mc = my * nz + mz
    me = mx * nyz + mc
    mesh_id = pl.DeviceIdType.MESH

    def device(x, c):
        return {"gx": x, "gy": c // nz, "gz": c % nz}

    def peer(d):
        return device(d // nyz, d % nyz)

    def inside(dx, dc):
        x, c = mx + dx, mc + dc
        return (x >= 0) & (x < nx) & (c >= 0) & (c < nyz)

    ind_copy = pltpu.make_async_copy(ind_hbm, ind, ind_sem)
    ind_copy.start()
    barrier = pltpu.get_barrier_semaphore()

    @pl.loop(1, owners)
    def _(k):
        pl.semaphore_signal(
            barrier, inc=1, device_id=peer((me + k) % owners), device_id_type=mesh_id)

    lane = lax.broadcasted_iota(jnp.int32, (CHUNK, LANES), 1)

    def chunk(q):
        return pl.ds(pl.multiple_of(q * CHUNK, CHUNK), CHUNK)

    def gather_columns(source, target):
        @pl.loop(0, ports // CHUNK)
        def _(q):
            for side, at in ((0, 0), (1, LANES - 1)):
                total = jnp.zeros((CHUNK, LANES), F32)
                for x in range(row_count):
                    total = jnp.where(lane == x, source[x, chunk(q)][:, at:at + 1], total)
                target[side, chunk(q)] = total.astype(target.dtype)

    steps = ((-1, 0, 0, 1), (1, 0, 1, 0), (0, -1, 0, 1), (0, 1, 1, 0))

    def edge(number, first_row, last_row, col_from, row_to, col_to, ssem, rsem):
        dx, dc, mine, theirs = steps[number]
        if dx:
            src, dst = (last_row if mine else first_row), row_to.at[theirs]
        else:
            src, dst = col_from.at[mine], col_to.at[theirs]
        return pltpu.make_async_remote_copy(
            src_ref=src, dst_ref=dst, send_sem=ssem.at[number], recv_sem=rsem.at[number],
            device_id=device(mx + dx, mc + dc), device_id_type=mesh_id)

    def stream_edge(number):
        return edge(number, stream_ref.at[0], stream_ref.at[row_count - 1], col_out, row_in, col_in,
                    edge_send, edge_recv)

    def field_edge(number):
        return edge(number, frow_out.at[0], frow_out.at[1], fcol_out, frow_in, fcol_in,
                    fedge_send, fedge_recv)

    all_rows, inner_cols = pl.ds(0, leaf_rows + 2), pl.ds(1, leaf_cols)
    plans = (
        (-1, 0, pl.ds(1, 1), inner_cols, pl.ds(leaf_rows + 1, 1), inner_cols),
        (1, 0, pl.ds(leaf_rows, 1), inner_cols, pl.ds(0, 1), inner_cols),
        (0, -1, all_rows, pl.ds(1, 1), all_rows, pl.ds(leaf_cols + 1, 1)),
        (0, 1, all_rows, pl.ds(leaf_cols, 1), all_rows, pl.ds(0, 1)),
    )

    def halo(number):
        dx, dc, src_r, src_c, dst_r, dst_c = plans[number]
        return pltpu.make_async_remote_copy(
            src_ref=bordered.at[src_r, src_c], dst_ref=bordered.at[dst_r, dst_c],
            send_sem=halo_send.at[number], recv_sem=halo_recv.at[number],
            device_id=device(mx + dx, mc + dc), device_id_type=mesh_id)

    def over(moves, test_sign, action, numbers=range(4)):
        for number in numbers:
            move = moves[number]

            @pl.when(inside(test_sign * move[0], test_sign * move[1]))
            def _():
                action(number)

    def exchange(src, dst, ssem, rsem, d, slot):
        return pltpu.make_async_remote_copy(
            src_ref=src.at[d], dst_ref=dst.at[slot], send_sem=ssem.at[d], recv_sem=rsem.at[slot],
            device_id=peer(d), device_id_type=mesh_id)

    own_cols = pl.ds(pl.multiple_of(mz * LANES, LANES), LANES)

    @pl.loop(0, ports // CHUNK)
    def _(q):
        for x in range(row_count):
            stream_ref[x, chunk(q)] = tile_ref[chunk(q), x, own_cols]

    gather_columns(stream_ref, col_out)
    for number, (dx, dc, _, theirs) in enumerate(steps):
        @pl.when(jnp.logical_not(inside(-dx, -dc)))
        def _():
            for target in ((row_in, frow_in) if dx else (col_in, fcol_in)):
                target[theirs] = jnp.zeros(target.shape[1:], target.dtype)
    for dx, dc, _, _, dst_r, dst_c in plans:
        @pl.when(jnp.logical_not(inside(-dx, -dc)))
        def _():
            view = bordered.at[dst_r, dst_c]
            view[...] = jnp.zeros(view.shape, BF)

    pl.semaphore_wait(barrier, owners - 1)

    over(steps, 1, lambda number: stream_edge(number).start())

    def send_blocks(k):
        to = (mx + nx - k) % nx * nyz

        @pl.loop(1 if isinstance(k, int) and k == 0 else 0, nyz)
        def _(i):
            d = to + (mc + i) % nyz
            exchange(ids_ref, got_ids, id_send, id_recv, d, me).start()
            exchange(send_ref, got, block_send, block_recv, d, me).start()

    send_blocks(0)
    if nx > 1:
        send_blocks(1)

    got[me] = send_ref[me]
    got_ids[me] = ids_ref[me]

    over(steps, -1, lambda number: stream_edge(number).wait_recv())

    for lr in range(leaf_rows):
        @pl.loop(0, ports // CHUNK)
        def _(q):
            def row(x):
                if x < 0:
                    return row_in[0, chunk(q)]
                if x >= row_count:
                    return row_in[1, chunk(q)]
                return stream_ref[x, chunk(q)]

            before, after = col_in[0, chunk(q)], col_in[1, chunk(q)]
            along_y, along_x = [], []
            for x in range(lr * LEAF_R, (lr + 1) * LEAF_R):
                left, right = sides(row(x), before[:, x:x + 1], after[:, x:x + 1])
                along_y.append(right - left)
                along_x.append(row(x - 1) - row(x + 1))
            for c, values in enumerate((along_y, along_x)):
                for j, value in enumerate(exchange_blocks(values)):
                    rounded = value.astype(BF)
                    bordered[lr + 1, j + 1, c, chunk(q)] = rounded
                    at = pl.multiple_of((lr * leaf_cols + j) * ports + q * CHUNK, CHUNK)
                    planes[pl.ds(at, CHUNK), c * LANES:(c + 1) * LANES] = rounded

    over(plans, 1, lambda number: halo(number).start(), (0, 1))

    @pl.loop(2, nx)
    def _(k):
        send_blocks(k)

    per_row = LANES // cap
    width = nyz * cap
    stack = 4
    tall = stack * ports

    def work_on_blocks(k):
        first = isinstance(k, int) and k == 0
        base = (mx + k) % nx * nyz

        @pl.loop(1 if first else 0, nyz)
        def _(i):
            s = base + (mc + i) % nyz
            exchange(ids_ref, got_ids, id_send, id_recv, s, s).wait_recv()
            exchange(send_ref, got, block_send, block_recv, s, s).wait_recv()

        rows = []
        for g in range(nyz // per_row):
            total = got_ids[base + g * per_row]
            for o in range(1, per_row):
                total = total + got_ids[base + g * per_row + o]
            rows.append(total)
        ids_row = jnp.concatenate(rows, axis=1) - 1.0
        block = got[pl.ds(base, nyz)]
        coupling = block[:, :, : 2 * LANES].reshape(width, 2 * LANES)
        current_t = block[:, :, 2 * LANES:].reshape(width, LANES).astype(F32).T.astype(BF)

        volt = jnp.zeros((ports, width), F32)
        for b in range(leaf_count // stack):
            part = lax.dot_general(
                planes[b * tall:(b + 1) * tall, :], coupling, (((1,), (1,)), ((), ())),
                preferred_element_type=F32)
            for i in range(stack):
                hit = ids_row == float(b * stack + i)
                volt = volt + jnp.where(hit, part[i * ports:(i + 1) * ports], 0.0)
        ret_send[pl.ds(base, nyz)] = volt.T.astype(BF).reshape(nyz, cap, LANES)

        @pl.loop(1 if first else 0, nyz)
        def _(i):
            d = base + (mc + i) % nyz
            exchange(ret_send, ret_ref, ret_ssem, ret_rsem, d, me).start()

        for b in range(leaf_count // stack):
            masked = jnp.concatenate(
                [jnp.where(ids_row == float(b * stack + i), current_t, jnp.zeros((), BF))
                 for i in range(stack)], axis=0)
            part = jnp.dot(masked, coupling, preferred_element_type=F32)
            if first:
                acc[b * tall:(b + 1) * tall, :] = part
            else:
                acc[b * tall:(b + 1) * tall, :] += part

    work_on_blocks(0)
    ret_ref[me] = ret_send[me]
    over(plans, -1, lambda number: halo(number).wait_recv(), (0, 1))
    over(plans, 1, lambda number: halo(number).start(), (2, 3))
    if nx > 1:
        work_on_blocks(1)

    over(plans, -1, lambda number: halo(number).wait_recv(), (2, 3))
    ind_copy.wait()

    @pl.loop(0, leaf_count)
    def _(l):
        r, j = l // leaf_cols, l % leaf_cols
        codes = [near_ref[r, j, n] for n in range(near_count)]
        at = pl.ds(pl.multiple_of(l * ports, ports), ports)
        for c in range(2):
            sources = jnp.concatenate(
                [bordered[r + code // 3, j + code % 3, c] for code in codes], axis=1)
            tiles = jnp.concatenate([ind[l, n, c] for n in range(near_count)], axis=1)
            acc[at, c * LANES:(c + 1) * LANES] += lax.dot_general(
                sources, tiles, (((1,), (1,)), ((), ())), preferred_element_type=F32)

    @pl.loop(2, nx)
    def _(k):
        work_on_blocks(k)

    for lr in range(leaf_rows):
        for c in range(2):
            @pl.loop(0, ports // CHUNK)
            def _(q):
                values = []
                for j in range(leaf_cols):
                    at = pl.multiple_of((lr * leaf_cols + j) * ports + q * CHUNK, CHUNK)
                    value = acc[pl.ds(at, CHUNK), c * LANES:(c + 1) * LANES]
                    values.append(value.astype(BF).astype(F32))
                for r, value in enumerate(exchange_blocks(values)):
                    grid[c, lr * LEAF_R + r, chunk(q)] = value

    frow_out[0] = grid[1, 0].astype(BF)
    frow_out[1] = grid[1, row_count - 1].astype(BF)
    gather_columns(grid.at[0], fcol_out)
    over(steps, 1, lambda number: field_edge(number).start())
    over(steps, -1, lambda number: field_edge(number).wait_recv())

    @pl.loop(0, ports // CHUNK)
    def _(q):
        def row(x):
            if x < 0:
                return frow_in[0, chunk(q)].astype(F32)
            if x >= row_count:
                return frow_in[1, chunk(q)].astype(F32)
            return grid[1, x, chunk(q)]

        before, after = fcol_in[0, chunk(q)].astype(F32), fcol_in[1, chunk(q)].astype(F32)
        for x in range(row_count):
            left, right = sides(grid[0, x, chunk(q)], before[:, x:x + 1], after[:, x:x + 1])
            loop_ref[chunk(q), x, :] = (left - right) + (row(x + 1) - row(x - 1))

    @pl.loop(1, owners)
    def _(k):
        s = (me + k) % owners
        exchange(ids_ref, got_ids, id_send, id_recv, s, s).wait_send()
        exchange(send_ref, got, block_send, block_recv, s, s).wait_send()
        exchange(ret_send, ret_ref, ret_ssem, ret_rsem, s, s).wait()

    over(steps, 1, lambda number: stream_edge(number).wait_send())
    over(steps, 1, lambda number: field_edge(number).wait_send())
    over(plans, 1, lambda number: halo(number).wait_send())


def body(stream, inductance, near_lists, filament_leaf, filament_current, filament_coupling):
    port_count = stream.shape[0]
    leaf_rows, leaf_cols, near_count, _, leaf_cells, _ = inductance.shape
    leaf_count = leaf_rows * leaf_cols
    nx, ny, nz = lax.axis_size("gx"), lax.axis_size("gy"), lax.axis_size("gz")
    owners = nx * ny * nz
    me = (lax.axis_index("gx") * ny + lax.axis_index("gy")) * nz + lax.axis_index("gz")

    row_count = stream.shape[1]
    filament_count = filament_leaf.shape[0]
    capacity = max(16, 2 * filament_count // owners)
    slot_count = owners * capacity
    plane_cols = leaf_cols * ny * nz
    leaf_row = filament_leaf // plane_cols
    leaf_col = filament_leaf % plane_cols
    owner_ids = leaf_row // leaf_rows * (ny * nz) + leaf_col // leaf_cols
    local_ids = leaf_row % leaf_rows * leaf_cols + leaf_col % leaf_cols
    owner_hits = owner_ids[:, None] == jnp.arange(owners, dtype=jnp.int32)[None, :]
    numbers = jnp.arange(filament_count, dtype=jnp.int32)
    earlier = (numbers[None, :] < numbers[:, None]).astype(BF)
    ranks = jnp.dot(earlier, owner_hits.astype(BF), preferred_element_type=F32)
    position = jnp.sum(jnp.where(owner_hits, ranks, 0.0), axis=1).astype(jnp.int32)
    target_slot = owner_ids * capacity + position
    placement_mask = target_slot[None, :] == jnp.arange(slot_count, dtype=jnp.int32)[:, None]
    placement = placement_mask.astype(BF)
    rows = jnp.concatenate(
        [filament_coupling.reshape(filament_count, 2 * leaf_cells), filament_current], axis=1)
    send = jnp.dot(placement, rows, preferred_element_type=F32).astype(BF)
    send = send.reshape(owners, capacity, 2 * leaf_cells + port_count)
    sent_leaf = jnp.max(jnp.where(placement_mask, local_ids[None, :] + 1, 0), axis=1).astype(F32)
    per_row = LANES // capacity
    lane_part = (jnp.arange(per_row, dtype=jnp.int32) == me % per_row).astype(F32)
    ids = (sent_leaf.reshape(owners, 1, capacity) * lane_part[None, :, None]).reshape(owners, 1, LANES)

    vmem = pl.BlockSpec(memory_space=pltpu.VMEM)
    dma = pltpu.SemaphoreType.DMA
    tile = (port_count, LANES)
    loop_voltage, returned = pl.pallas_call(
        functools.partial(kernel, (nx, ny, nz)),
        out_shape=(
            jax.ShapeDtypeStruct((port_count, row_count, LANES), F32),
            jax.ShapeDtypeStruct((owners, capacity, port_count), BF),
        ),
        in_specs=[pl.BlockSpec(memory_space=pltpu.SMEM), vmem, vmem, vmem,
                  pl.BlockSpec(memory_space=pl.ANY)],
        out_specs=(vmem, vmem),
        scratch_shapes=[
            pltpu.VMEM((row_count,) + tile, F32),
            pltpu.VMEM((leaf_rows + 2, leaf_cols + 2, 2, port_count, leaf_cells), BF),
            pltpu.VMEM((leaf_count * port_count, 2 * leaf_cells), BF),
            pltpu.VMEM(send.shape, BF),
            pltpu.VMEM(ids.shape, F32),
            pltpu.VMEM((leaf_count, near_count, 2, leaf_cells, leaf_cells), BF),
            pltpu.VMEM((leaf_count * port_count, 2 * leaf_cells), F32),
            pltpu.VMEM((owners, capacity, port_count), BF),
            pltpu.VMEM((2, row_count) + tile, F32),
            pltpu.VMEM((2,) + tile, F32), pltpu.VMEM((2,) + tile, F32), pltpu.VMEM((2,) + tile, F32),
            pltpu.VMEM((2,) + tile, BF), pltpu.VMEM((2,) + tile, BF),
            pltpu.VMEM((2,) + tile, BF), pltpu.VMEM((2,) + tile, BF),
            dma, dma((4,)), dma((4,)), dma((4,)), dma((4,)), dma((4,)), dma((4,)),
            dma((owners,)), dma((owners,)), dma((owners,)), dma((owners,)),
            dma((owners,)), dma((owners,)),
        ],
        compiler_params=pltpu.CompilerParams(
            collective_id=0, has_side_effects=True, vmem_limit_bytes=56 * 2**20),
        cost_estimate=pl.CostEstimate(
            flops=3 * 2 * 2**29, bytes_accessed=12 * 2**20, transcendentals=0),
    )(near_lists, stream, send, ids,
      inductance.reshape(leaf_count, near_count, 2, leaf_cells, leaf_cells))

    filament_voltage = lax.dot_general(
        placement, returned.reshape(slot_count, port_count), (((0,), (0,)), ((), ())),
        preferred_element_type=F32).astype(BF)
    return (loop_voltage, filament_voltage)


def solution(mesh):
    return jax.shard_map(
        body,
        mesh=mesh,
        in_specs=(
            P("groups", "gx", "gy"),
            P(("groups", "gx"), ("gy", "gz"), None, None, None, None),
            P(("groups", "gx"), ("gy", "gz"), None),
            P(("groups", "gx", "gy", "gz")),
            P(("groups", "gx", "gy", "gz"), None),
            P(("groups", "gx", "gy", "gz"), None, None),
        ),
        out_specs=(P("groups", "gx", ("gy", "gz")), P(("groups", "gx", "gy", "gz"), None)),
        check_vma=False,
    )
```

time: 98.4 us -> 73.6 us (0.75)
  the two profiles are of different devices: /device:TPU:0 before, /device:TPU:1 now
where the time goes in v2:
time: 73.6 us; the launch traced here: 73.3 us
  Pallas kernels  62.2 us (85%)
  matrix products  5.15 us (7%)
  local copies, waits for them, and re-layouts  3.57 us (5%)
  other arithmetic  1.68 us (2%)
    pallas_call x1, Pallas kernels, body(): pl.pallas_call(functools.partial(kernel, (nx, ny, nz)), out_shape=(jax.Sh...  62.2 us
    unnamed x2, local copies, waits for them, and re-layouts  3.25 us
    dot_general x1, matrix products, body(): send = jnp.dot(placement, rows, preferred_element_type=F32).astype(BF)  2.5 us
    dot_general x1, matrix products, body(): lax.dot_general(placement, returned.reshape(slot_count, port_count), (((0...  2.38 us

profile of v2, /device:TPU:1, one launch (start us, length us, event | category | flops | bytes accessed | tf_op | source)
XLA Modules:
  0.0 73.3 jit_solution(6492070265291954183)
XLA Ops:
  0.7 0.1 mul.57
  0.7 0.1 mul.58
  0.8 0.7 fusion.15
  1.5 0.3 fusion.4
  1.8 0.4 select_reduce_fusion
  2.2 0.1 convert_element_type.32
  2.2 0.1 mul.54
  2.3 0.6 broadcast_multiply_fusion.ids_ref
  2.9 1.0 %copy.10 = bf16[64,8,2,128]{3,1,2,0:T(8,128)(2,1)S(1)} copy(bf16[64,8,2,128]{3,2,1,0:T(2,128)(2,1)} %bitcast.8) | data formatting | bytes 524288
  3.9 2.5 %fusion.2 = bf16[1024,384]{1,0:T(8,128)(2,1)} fusion(s32[512]{0:T(512)S(1)} %convert_add_fusion, bf16[512,128]{1,0:T(8,128)(2,1)} %param.10, bf16[512,256]{1,0:T(8,128)(2,1)S(1)} %bitcast.9), kind=kOutput, calls=%fused_computation.4 | convolution fusion | flops 404357120 | bytes 1181696 | tf_op jit(solution)/shard_map/dot_general | solution.py:361
  6.4 62.2 %shard_map.77 = (f32[128,16,128]{2,1,0:T(8,128)}, bf16[16,64,128]{2,1,0:T(8,128)(2,1)}) custom-call(s32[2,8,8]{2,1,0:T(8,128)} %near_ref.1, f32[128,16,256]{2,1,0:T(8,128)} %tile_ref.1, bf16[16,64,384]{2,1,0:T(8,128)(2,1)} %bitcast.11, f32[16,1,128]{2,1,0:T(1,128)} %broadcast_multiply_fusion.ids_ref, bf16[16,8,2,128,128]{4,3,2,1,0:T(8,128)(2,1)} %bitcast.10), custom_call_target="tpu_custom_call" | custom-call | flops 3221225472 | bytes 12582912 | tf_op jit(solution)/shard_map/pallas_call | solution.py:371
  68.7 2.4 %fusion.3 = bf16[512,128]{1,0:T(8,128)(2,1)} fusion(bf16[1024,128]{1,0:T(8,128)(2,1)} %bitcast.12, s32[512]{0:T(512)S(1)} %convert_add_fusion), kind=kOutput, calls=%fused_computation.5 | convolution fusion | flops 134807552 | bytes 395264 | tf_op jit(solution)/shard_map/dot_general | solution.py:404
  71.1 2.3 %copy.12 = f32[128,16,128]{2,1,0:T(8,128)} copy(f32[128,16,128]{2,1,0:T(8,128)} %get-tuple-element.10) | data formatting | bytes 2097152
  (4 shorter events, 0.0 us)

commit v3 on v2

--- a/solution.py
+++ b/solution.py
@@ -112,13 +112,16 @@
         return edge(number, frow_out.at[0], frow_out.at[1], fcol_out, frow_in, fcol_in,
                     fedge_send, fedge_recv)
 
-    all_rows, inner_cols = pl.ds(0, leaf_rows + 2), pl.ds(1, leaf_cols)
-    plans = (
-        (-1, 0, pl.ds(1, 1), inner_cols, pl.ds(leaf_rows + 1, 1), inner_cols),
-        (1, 0, pl.ds(leaf_rows, 1), inner_cols, pl.ds(0, 1), inner_cols),
-        (0, -1, all_rows, pl.ds(1, 1), all_rows, pl.ds(leaf_cols + 1, 1)),
-        (0, 1, all_rows, pl.ds(leaf_cols, 1), all_rows, pl.ds(0, 1)),
-    )
+    every_r, every_c = pl.ds(1, leaf_rows), pl.ds(1, leaf_cols)
+    plans = []
+    for dx in (-1, 0, 1):
+        for dc in (-1, 0, 1):
+            if dx or dc:
+                src_r = every_r if dx == 0 else pl.ds(1 if dx < 0 else leaf_rows, 1)
+                dst_r = every_r if dx == 0 else pl.ds(leaf_rows + 1 if dx < 0 else 0, 1)
+                src_c = every_c if dc == 0 else pl.ds(1 if dc < 0 else leaf_cols, 1)
+                dst_c = every_c if dc == 0 else pl.ds(leaf_cols + 1 if dc < 0 else 0, 1)
+                plans.append((dx, dc, src_r, src_c, dst_r, dst_c))
 
     def halo(number):
         dx, dc, src_r, src_c, dst_r, dst_c = plans[number]
@@ -127,10 +130,8 @@
             send_sem=halo_send.at[number], recv_sem=halo_recv.at[number],
             device_id=device(mx + dx, mc + dc), device_id_type=mesh_id)
 
-    def over(moves, test_sign, action, numbers=range(4)):
-        for number in numbers:
-            move = moves[number]
-
+    def over(moves, test_sign, action):
+        for number, move in enumerate(moves):
             @pl.when(inside(test_sign * move[0], test_sign * move[1]))
             def _():
                 action(number)
@@ -172,9 +173,10 @@
             exchange(ids_ref, got_ids, id_send, id_recv, d, me).start()
             exchange(send_ref, got, block_send, block_recv, d, me).start()
 
+    far = nx // 2
     send_blocks(0)
-    if nx > 1:
-        send_blocks(1)
+    if far:
+        send_blocks(far)
 
     got[me] = send_ref[me]
     got_ids[me] = ids_ref[me]
@@ -204,11 +206,13 @@
                     at = pl.multiple_of((lr * leaf_cols + j) * ports + q * CHUNK, CHUNK)
                     planes[pl.ds(at, CHUNK), c * LANES:(c + 1) * LANES] = rounded
 
-    over(plans, 1, lambda number: halo(number).start(), (0, 1))
-
-    @pl.loop(2, nx)
-    def _(k):
-        send_blocks(k)
+    over(plans, 1, lambda number: halo(number).start())
+
+    def over_rest(action):
+        pl.loop(1, far)(action)
+        pl.loop(far + 1, nx)(action)
+
+    over_rest(send_blocks)
 
     per_row = LANES // cap
     width = nyz * cap
@@ -263,12 +267,10 @@
 
     work_on_blocks(0)
     ret_ref[me] = ret_send[me]
-    over(plans, -1, lambda number: halo(number).wait_recv(), (0, 1))
-    over(plans, 1, lambda number: halo(number).start(), (2, 3))
-    if nx > 1:
-        work_on_blocks(1)
-
-    over(plans, -1, lambda number: halo(number).wait_recv(), (2, 3))
+    if far:
+        work_on_blocks(far)
+
+    over(plans, -1, lambda number: halo(number).wait_recv())
     ind_copy.wait()
 
     @pl.loop(0, leaf_count)
@@ -283,9 +285,7 @@
             acc[at, c * LANES:(c + 1) * LANES] += lax.dot_general(
                 sources, tiles, (((1,), (1,)), ((), ())), preferred_element_type=F32)
 
-    @pl.loop(2, nx)
-    def _(k):
-        work_on_blocks(k)
+    over_rest(work_on_blocks)
 
     for lr in range(leaf_rows):
         for c in range(2):
@@ -317,7 +317,7 @@
         before, after = fcol_in[0, chunk(q)].astype(F32), fcol_in[1, chunk(q)].astype(F32)
         for x in range(row_count):
             left, right = sides(grid[0, x, chunk(q)], before[:, x:x + 1], after[:, x:x + 1])
-            loop_ref[chunk(q), x, :] = (left - right) + (row(x + 1) - row(x - 1))
+            loop_ref[x, chunk(q)] = (left - right) + (row(x + 1) - row(x - 1))
 
     @pl.loop(1, owners)
     def _(k):
@@ -368,10 +368,10 @@
     vmem = pl.BlockSpec(memory_space=pltpu.VMEM)
     dma = pltpu.SemaphoreType.DMA
     tile = (port_count, LANES)
-    loop_voltage, returned = pl.pallas_call(
+    loop_rows, returned = pl.pallas_call(
         functools.partial(kernel, (nx, ny, nz)),
         out_shape=(
-            jax.ShapeDtypeStruct((port_count, row_count, LANES), F32),
+            jax.ShapeDtypeStruct((row_count,) + tile, F32),
             jax.ShapeDtypeStruct((owners, capacity, port_count), BF),
         ),
         in_specs=[pl.BlockSpec(memory_space=pltpu.SMEM), vmem, vmem, vmem,
@@ -390,7 +390,7 @@
             pltpu.VMEM((2,) + tile, F32), pltpu.VMEM((2,) + tile, F32), pltpu.VMEM((2,) + tile, F32),
             pltpu.VMEM((2,) + tile, BF), pltpu.VMEM((2,) + tile, BF),
             pltpu.VMEM((2,) + tile, BF), pltpu.VMEM((2,) + tile, BF),
-            dma, dma((4,)), dma((4,)), dma((4,)), dma((4,)), dma((4,)), dma((4,)),
+            dma, dma((8,)), dma((8,)), dma((4,)), dma((4,)), dma((4,)), dma((4,)),
             dma((owners,)), dma((owners,)), dma((owners,)), dma((owners,)),
             dma((owners,)), dma((owners,)),
         ],
@@ -404,7 +404,7 @@
     filament_voltage = lax.dot_general(
         placement, returned.reshape(slot_count, port_count), (((0,), (0,)), ((), ())),
         preferred_element_type=F32).astype(BF)
-    return (loop_voltage, filament_voltage)
+    return (loop_rows.transpose(1, 0, 2), filament_voltage)
 
 
 def solution(mesh):

time: 73.6 us -> 67.8 us (0.921)
  the two profiles are of different devices: /device:TPU:1 before, /device:TPU:0 now
where the time goes in v3:
time: 67.8 us; the launch traced here: 67.6 us
  Pallas kernels  56.8 us (84%)
  matrix products  4.2 us (6%)
  local copies, waits for them, and re-layouts  4.16 us (6%)
  other arithmetic  1.68 us (2%)
  between operations  0.69 us (1%)
    pallas_call x1, Pallas kernels, body(): pl.pallas_call(functools.partial(kernel, (nx, ny, nz)), out_shape=(jax.Sh...  56.8 us
    unnamed x4, local copies, waits for them, and re-layouts  3.84 us
    dot_general x1, matrix products, body(): send = jnp.dot(placement, rows, preferred_element_type=F32).astype(BF)  2.5 us
    dot_general x1, matrix products, body(): lax.dot_general(placement, returned.reshape(slot_count, port_count), (((0...  1.43 us

profile of v3, /device:TPU:0, one launch (start us, length us, event | category | flops | bytes accessed | tf_op | source)
XLA Modules:
  0.0 67.6 jit_solution(13810831669558914384)
XLA Ops:
  0.7 0.1 mul.57
  0.7 0.1 mul.58
  0.8 0.7 %fusion.15 = (s32[512]{0:T(512)S(1)}, s32[512]{0:T(512)S(1)}) fusion(s32[512]{0:T(512)} %param.9), kind=kLoop, calls=%fused_computation.37 | loop fusion | flops 31744 | bytes 6144 | tf_op jit(solution)/shard_map/add | solution.py:363
  1.5 0.3 fusion.4
  1.8 0.4 select_reduce_fusion
  2.2 0.1 convert_element_type.32
  2.2 0.1 mul.54
  2.3 0.6 broadcast_multiply_fusion.ids_ref
  2.9 1.0 %copy.12 = bf16[64,8,2,128]{3,1,2,0:T(8,128)(2,1)S(1)} copy(bf16[64,8,2,128]{3,2,1,0:T(2,128)(2,1)} %bitcast.10) | data formatting | bytes 524288
  3.9 2.5 %fusion.2 = bf16[1024,384]{1,0:T(8,128)(2,1)} fusion(s32[512]{0:T(512)S(1)} %convert_add_fusion, bf16[512,128]{1,0:T(8,128)(2,1)} %param.10, bf16[512,256]{1,0:T(8,128)(2,1)S(1)} %bitcast.11), kind=kOutput, calls=%fused_computation.4 | convolution fusion | flops 404357120 | bytes 1181696 | tf_op jit(solution)/shard_map/dot_general | solution.py:361
  6.4 56.8 %shard_map.77 = (f32[16,128,128]{2,1,0:T(8,128)}, bf16[16,64,128]{2,1,0:T(8,128)(2,1)}) custom-call(s32[2,8,8]{2,1,0:T(8,128)} %near_ref.1, f32[128,16,256]{2,1,0:T(8,128)} %tile_ref.1, bf16[16,64,384]{2,1,0:T(8,128)(2,1)} %bitcast.13, f32[16,1,128]{2,1,0:T(1,128)} %broadcast_multiply_fusion.ids_ref, bf16[16,8,2,128,128]{4,3,2,1,0:T(8,128)(2,1)} %bitcast.12), custom_call_target="tpu_custom_call" | custom-call | flops 3221225472 | bytes 12582912 | tf_op jit(solution)/shard_map/pallas_call | solution.py:371
  63.3 0.0 copy-start
  63.3 2.8 %copy.9 = f32[128,16,128]{2,1,0:T(8,128)} copy(f32[128,16,128]{2,0,1:T(8,128)} %bitcast.9) | data formatting | bytes 2097152
  66.1 0.0 copy-done
  66.1 1.4 %fusion.3 = bf16[512,128]{1,0:T(8,128)(2,1)} fusion(bf16[1024,128]{1,0:T(8,128)(2,1)S(1)} %bitcast.14, s32[512]{0:T(512)S(1)} %convert_add_fusion), kind=kOutput, calls=%fused_computation.5 | convolution fusion | flops 134807552 | bytes 395264 | tf_op jit(solution)/shard_map/dot_general | solution.py:404
  (4 shorter events, 0.0 us)
Async XLA Ops:
  63.3 2.9 %copy-start = (bf16[16,64,128]{2,1,0:T(8,128)(2,1)S(1)}, bf16[16,64,128]{2,1,0:T(8,128)(2,1)}, u32[]{:S(2)}) copy-start(bf16[16,64,128]{2,1,0:T(8,128)(2,1)} %get-tuple-element.5) | copy-start | bytes 786436

commit v4 on v3

--- a/solution.py
+++ b/solution.py
@@ -40,8 +40,8 @@
 
 
 def kernel(
-    dims, near_ref, tile_ref, send_ref, ids_ref, ind_hbm, loop_ref, ret_ref,
-    stream_ref, bordered, planes, got, got_ids, ind, acc, ret_send, grid,
+    dims, near_ref, tile_ref, slot_ref, coupling_ref, current_ref, ids_ref, ind_hbm, loop_ref, ret_ref,
+    send_ref, stream_ref, bordered, planes, got, got_ids, ind, acc, ret_send, grid,
     col_out, row_in, col_in, frow_out, fcol_out, frow_in, fcol_in,
     ind_sem, halo_send, halo_recv, edge_send, edge_recv, fedge_send, fedge_recv,
     block_send, block_recv, id_send, id_recv, ret_ssem, ret_rsem,
@@ -140,6 +140,19 @@
         return pltpu.make_async_remote_copy(
             src_ref=src.at[d], dst_ref=dst.at[slot], send_sem=ssem.at[d], recv_sem=rsem.at[slot],
             device_id=peer(d), device_id_type=mesh_id)
+
+    group = 2 * LANES
+    group_owners = group // cap
+
+    @pl.loop(0, owners // group_owners)
+    def _(g):
+        row = lax.broadcasted_iota(jnp.int32, (group, slot_ref.shape[1]), 0) + g * group
+        mask = jnp.where(row == slot_ref[...], 1.0, 0.0).astype(BF)
+        to = pl.ds(g * group_owners, group_owners)
+        coupled = jnp.dot(mask, coupling_ref[...], preferred_element_type=F32).astype(BF)
+        driven = jnp.dot(mask, current_ref[...], preferred_element_type=F32).astype(BF)
+        send_ref[to, :, : 2 * LANES] = coupled.reshape(group_owners, cap, 2 * LANES)
+        send_ref[to, :, 2 * LANES:] = driven.reshape(group_owners, cap, LANES)
 
     own_cols = pl.ds(pl.multiple_of(mz * LANES, LANES), LANES)
 
@@ -356,10 +369,6 @@
     target_slot = owner_ids * capacity + position
     placement_mask = target_slot[None, :] == jnp.arange(slot_count, dtype=jnp.int32)[:, None]
     placement = placement_mask.astype(BF)
-    rows = jnp.concatenate(
-        [filament_coupling.reshape(filament_count, 2 * leaf_cells), filament_current], axis=1)
-    send = jnp.dot(placement, rows, preferred_element_type=F32).astype(BF)
-    send = send.reshape(owners, capacity, 2 * leaf_cells + port_count)
     sent_leaf = jnp.max(jnp.where(placement_mask, local_ids[None, :] + 1, 0), axis=1).astype(F32)
     per_row = LANES // capacity
     lane_part = (jnp.arange(per_row, dtype=jnp.int32) == me % per_row).astype(F32)
@@ -368,20 +377,22 @@
     vmem = pl.BlockSpec(memory_space=pltpu.VMEM)
     dma = pltpu.SemaphoreType.DMA
     tile = (port_count, LANES)
+    block_shape = (owners, capacity, 2 * leaf_cells + port_count)
     loop_rows, returned = pl.pallas_call(
         functools.partial(kernel, (nx, ny, nz)),
         out_shape=(
             jax.ShapeDtypeStruct((row_count,) + tile, F32),
             jax.ShapeDtypeStruct((owners, capacity, port_count), BF),
         ),
-        in_specs=[pl.BlockSpec(memory_space=pltpu.SMEM), vmem, vmem, vmem,
+        in_specs=[pl.BlockSpec(memory_space=pltpu.SMEM), vmem, vmem, vmem, vmem, vmem,
                   pl.BlockSpec(memory_space=pl.ANY)],
         out_specs=(vmem, vmem),
         scratch_shapes=[
+            pltpu.VMEM(block_shape, BF),
             pltpu.VMEM((row_count,) + tile, F32),
             pltpu.VMEM((leaf_rows + 2, leaf_cols + 2, 2, port_count, leaf_cells), BF),
             pltpu.VMEM((leaf_count * port_count, 2 * leaf_cells), BF),
-            pltpu.VMEM(send.shape, BF),
+            pltpu.VMEM(block_shape, BF),
             pltpu.VMEM(ids.shape, F32),
             pltpu.VMEM((leaf_count, near_count, 2, leaf_cells, leaf_cells), BF),
             pltpu.VMEM((leaf_count * port_count, 2 * leaf_cells), F32),
@@ -398,7 +409,8 @@
             collective_id=0, has_side_effects=True, vmem_limit_bytes=56 * 2**20),
         cost_estimate=pl.CostEstimate(
             flops=3 * 2 * 2**29, bytes_accessed=12 * 2**20, transcendentals=0),
-    )(near_lists, stream, send, ids,
+    )(near_lists, stream, target_slot.reshape(1, filament_count),
+      filament_coupling.reshape(filament_count, 2 * leaf_cells), filament_current, ids,
       inductance.reshape(leaf_count, near_count, 2, leaf_cells, leaf_cells))
 
     filament_voltage = lax.dot_general(

time: 67.8 us -> 65.9 us (0.972)
  matrix products: 4.2 us -> 1.7 us
  local copies, waits for them, and re-layouts: 4.16 us -> 4.87 us
    dot_general x1 -> x0, matrix products: 2.5 us -> none  [body(): send = jnp.dot(placement, rows, preferred_element_type=F32).astype(BF)]
    unnamed x4 -> x8, local copies, waits for them, and re-layouts: 3.84 us -> 4.55 us
where the time goes in v4:
time: 65.9 us; the launch traced here: 65.7 us
  Pallas kernels  56.7 us (86%)
  local copies, waits for them, and re-layouts  4.87 us (7%)
  matrix products  1.7 us (3%)
  other arithmetic  1.68 us (3%)
  between operations  0.71 us (1%)
    pallas_call x1, Pallas kernels, body(): pl.pallas_call(functools.partial(kernel, (nx, ny, nz)), out_shape=(jax.Sh...  56.7 us
    unnamed x8, local copies, waits for them, and re-layouts  4.55 us
    dot_general x1, matrix products, body(): lax.dot_general(placement, returned.reshape(slot_count, port_count), (((0...  1.43 us

profile of v4, /device:TPU:0, one launch (start us, length us, event | category | flops | bytes accessed | tf_op | source)
XLA Modules:
  0.0 65.7 jit_solution(8748423699427072858)
XLA Ops:
  0.7 0.1 mul.57
  0.7 0.1 mul.58
  0.8 0.7 %fusion.9 = (s32[512]{0:T(512)S(1)}, s32[512]{0:T(512)S(1)}) fusion(s32[512]{0:T(512)} %param.9), kind=kLoop, calls=%fused_computation.31 | loop fusion | flops 31744 | bytes 6144 | tf_op jit(solution)/shard_map/add | solution.py:372
  1.5 0.3 fusion.2
  1.8 0.0 copy-start
  1.8 0.4 select_reduce_fusion
  2.2 0.1 convert_element_type.28
  2.3 0.1 mul.54
  2.3 0.6 broadcast_multiply_fusion.ids_ref
  2.9 1.7 %copy.12 = bf16[64,8,2,128]{3,1,2,0:T(8,128)(2,1)} copy(bf16[64,8,2,128]{3,2,1,0:T(2,128)(2,1)} %bitcast.10) | data formatting | bytes 524288
  4.6 0.0 copy-done
  4.6 56.7 %shard_map.77 = (f32[16,128,128]{2,1,0:T(8,128)}, bf16[16,64,128]{2,1,0:T(8,128)(2,1)}) custom-call(s32[2,8,8]{2,1,0:T(8,128)} %near_ref.1, f32[128,16,256]{2,1,0:T(8,128)} %tile_ref.1, s32[1,512]{1,0:T(1,128)} %bitcast.12, bf16[512,256]{1,0:T(8,128)(2,1)} %bitcast.11, bf16[512,128]{1,0:T(8,128)(2,1)} %current_ref.1, ...), custom_call_target="tpu_custom_call" | custom-call | flops 3221225472 | bytes 12582912 | tf_op jit(solution)/shard_map/pallas_call | solution.py:381
  61.4 0.0 copy-start.1
  61.4 0.0 copy-start.2
  61.4 2.8 %copy.9 = f32[128,16,128]{2,1,0:T(8,128)} copy(f32[128,16,128]{2,0,1:T(8,128)} %bitcast.9) | data formatting | bytes 2097152
  64.2 0.0 copy-done.1
  64.2 0.0 copy-done.2
  64.2 1.4 %fusion.1 = bf16[512,128]{1,0:T(8,128)(2,1)} fusion(bf16[1024,128]{1,0:T(8,128)(2,1)S(1)} %bitcast.14, s32[512]{0:T(512)S(1)} %copy-done.1), kind=kOutput, calls=%fused_computation.3 | convolution fusion | flops 134807552 | bytes 395264 | tf_op jit(solution)/shard_map/dot_general | solution.py:416
  (4 shorter events, 0.0 us)
Async XLA Ops:
  1.8 2.8 %copy-start = (s32[512]{0:T(512)}, s32[512]{0:T(512)S(1)}, u32[]{:S(2)}) copy-start(s32[512]{0:T(512)S(1)} %convert_add_fusion) | copy-start | bytes 6148
  61.4 2.9 %copy-start.1 = (s32[512]{0:T(512)S(1)}, s32[512]{0:T(512)}, u32[]{:S(2)}) copy-start(s32[512]{0:T(512)} %copy-done) | copy-start | bytes 6148
  61.4 2.9 %copy-start.2 = (bf16[16,64,128]{2,1,0:T(8,128)(2,1)S(1)}, bf16[16,64,128]{2,1,0:T(8,128)(2,1)}, u32[]{:S(2)}) copy-start(bf16[16,64,128]{2,1,0:T(8,128)(2,1)} %get-tuple-element.5) | copy-start | bytes 786436
